TPU v7x, 512 devices: a whole 4x8x8 slice. The times are simulated.
512 devices in a mesh: elec: 16 (over x, y_hi), tm: 32 (over y_lo, z, core).
Axes of the slice: x: 4, y: 8 (y_hi: 4, y_lo: 2; y = y_hi * 2 + y_lo), z: 8, core: 2. Of those that a mesh axis runs over, the one named last changes fastest.
Arguments:
- signals: bfloat16 [4096, 12288], P('elec', 'tm'), may hold values from -6 to 6
- vectors: bfloat16 [128, 65536], P(None, 'elec'), may hold values from -0.0234375 to 0.0234375
Outputs:
- sources: bfloat16 [128, 12288], P(None, 'tm')
- unmixing: float32 [128, 65536], P(None, ('elec', 'tm'))
All inputs are finite; a program needn't handle non-finite values.
Results may differ from a plain program's by a relative error of at most 0.004.
Values may be sent and summed in bfloat16 or wider, within the bound.
A program may use at most 64 MiB of HBM per device.

v0:
```python
import math

import jax
import jax.numpy as jnp
from jax import lax
from jax.sharding import PartitionSpec as P

LAGS = 16
NS_STEPS = 6


START = 0.15


def from_behind(block, axis, distance):
    devices = range(lax.axis_size(axis))
    route = [(i - distance, i) for i in devices if i - distance in devices]
    return lax.ppermute(block, axis, route)


def shifted(padded, offset, length):
    return lax.slice_in_dim(padded, LAGS - 1 - offset, LAGS - 1 - offset + length, axis=1)


def combine(reduced, own_vectors, deriv_mean, samples_total):
    return reduced / samples_total - deriv_mean[:, None] * own_vectors.astype(jnp.float32)


def orthogonal(columns, total_norm, total_gram):
    rows_count = columns.shape[0]
    squares = total_norm(jnp.sum(columns * columns))
    current = columns * (START * math.sqrt(rows_count) * lax.rsqrt(squares + 1e-06))
    for iteration in range(NS_STEPS):
        gram = total_gram(
            lax.dot_general(
                current,
                current,
                (((1,), (1,)), ((), ())),
                precision=lax.Precision.HIGHEST,
                preferred_element_type=jnp.float32,
            )
        )
        current = 1.5 * current - 0.5 * jnp.dot(gram, current, precision=lax.Precision.HIGHEST)
    return current


def shards(signals, vectors):
    elec_count, length = signals.shape
    vec_count = vectors.shape[0]
    prior_tail = from_behind(signals[:, length - LAGS :], "tm", 1)
    padded = jnp.concatenate([prior_tail[:, 1:], signals], axis=1)
    weights = vectors.reshape(vec_count, elec_count, LAGS)
    partial_sums = jnp.zeros((vec_count, length), jnp.float32)
    for offset in range(LAGS):
        partial_sums = partial_sums + jnp.dot(
            weights[:, :, offset],
            shifted(padded, offset, length),
            preferred_element_type=jnp.float32,
        )
    source_sums = lax.psum(partial_sums, "elec")
    cubed = (source_sums * source_sums * source_sums).astype(jnp.bfloat16)
    deriv_local = jnp.sum(3.0 * source_sums * source_sums, axis=1)
    pieces = []
    for offset in range(LAGS):
        pieces.append(
            lax.dot_general(
                cubed,
                shifted(padded, offset, length),
                (((1,), (1,)), ((), ())),
                preferred_element_type=jnp.float32,
            )
        )
    gradient_term = jnp.stack(pieces, axis=2).reshape(vec_count, elec_count * LAGS)
    samples_total = length * lax.axis_size("tm")
    deriv_mean = lax.psum(deriv_local, "tm") / samples_total
    reduced = lax.psum(gradient_term, "tm")
    updated = combine(reduced, vectors, deriv_mean, samples_total)

    def norm_elec(value):
        return lax.psum(value, "elec")

    def gram_elec(value):
        return lax.psum(value.astype(jnp.bfloat16), "elec").astype(jnp.float32)

    whole_block = orthogonal(updated, norm_elec, gram_elec)
    width = whole_block.shape[1] // lax.axis_size("tm")
    result = lax.dynamic_slice_in_dim(whole_block, lax.axis_index("tm") * width, width, 1)
    return (source_sums.astype(jnp.bfloat16), result)


def solution(mesh):
    return jax.shard_map(
        shards,
        mesh=mesh,
        in_specs=(P("elec", "tm"), P(None, "elec")),
        out_specs=(P(None, "tm"), P(None, ("elec", "tm"))),
        check_vma=False,
    )
```

profile of v0, /device:TPU:8, one launch (start us, length us, event | category | flops | bytes accessed | tf_op | source)
XLA Modules:
  0.0 991.5 jit_solution(11437464873327117757)
XLA Ops:
  8.1 1.9 collective-permute-start
  11.7 2.3 fusion.106
  15.9 4.4 collective-permute-done
  25.9 164.5 %all-reduce.3.cloned.1.call-done = f32[128,384]{1,0:T(8,128)} async-done(((f32[128,384]{1,0:T(8,128)}), f32[128,384]{1,0:T(8,128)}) %all-reduce.3.cloned.1.call-update) | async-done | bytes 196624 | tf_op jit(solution)/shard_map/psum | solution.py:60
  207.2 2.2 copy.51
  209.5 1.8 copy.52
  211.3 53.7 %psum.72 = f32[128]{0:T(128)S(1)} all-reduce(f32[128]{0:T(128)S(1)} %get-tuple-element.19), channel_id=1, replica_groups=mesh['elec'=16,'tm'=32] {'tm'}, use_global_device_ids=true, to_apply=%region_3.0 | all-reduce | flops 128 | bytes 1024 | tf_op jit(solution)/shard_map/psum | solution.py:75
  265.0 177.4 %all-reduce.5.cloned.1.call-done = f32[128,4096]{1,0:T(8,128)} async-done(((f32[128,4096]{1,0:T(8,128)}), f32[128,4096]{1,0:T(8,128)}) %all-reduce.5.cloned.1.call-update) | async-done | bytes 2097168 | tf_op jit(solution)/shard_map/psum | solution.py:76
  442.4 3.0 multiply_reduce_fusion
  445.4 45.7 %psum.73 = f32[]{:T(128)} all-reduce(f32[]{:T(128)} %multiply_reduce_fusion), channel_id=1, replica_groups=mesh['elec'=16,'tm'=32] {'elec'}, use_global_device_ids=true, to_apply=%region_5.0 | all-reduce | flops 1 | bytes 8 | tf_op jit(solution)/shard_map/psum | solution.py:80
  491.8 2.5 fusion.38
  494.3 76.8 %psum.74 = bf16[128,128]{1,0:T(8,128)(2,1)S(1)} all-reduce(bf16[128,128]{1,0:T(8,128)(2,1)S(1)} %fusion.38), channel_id=1, replica_groups=mesh['elec'=16,'tm'=32] {'elec'}, use_global_device_ids=true, to_apply=%region_6.0 | all-reduce | flops 16384 | bytes 65536 | tf_op jit(solution)/shard_map/psum | solution.py:83
  571.1 2.2 fusion.4
  576.5 76.8 %psum.75 = bf16[128,128]{1,0:T(8,128)(2,1)S(1)} all-reduce(bf16[128,128]{1,0:T(8,128)(2,1)S(1)} %convolution_convert_fusion.4), channel_id=1, replica_groups=mesh['elec'=16,'tm'=32] {'elec'}, use_global_device_ids=true, to_apply=%region_7.0 | all-reduce | flops 16384 | bytes 65536 | tf_op jit(solution)/shard_map/psum | solution.py:83
  653.3 3.6 fusion.3
  656.9 1.8 convolution_convert_fusion.3
  658.7 77.0 %psum.76 = bf16[128,128]{1,0:T(8,128)(2,1)S(1)} all-reduce(bf16[128,128]{1,0:T(8,128)(2,1)S(1)} %convolution_convert_fusion.3), channel_id=1, replica_groups=mesh['elec'=16,'tm'=32] {'elec'}, use_global_device_ids=true, to_apply=%region_8.0 | all-reduce | flops 16384 | bytes 65536 | tf_op jit(solution)/shard_map/psum | solution.py:83
  738.5 1.8 convolution_convert_fusion.2
  740.3 76.8 %psum.77 = bf16[128,128]{1,0:T(8,128)(2,1)S(1)} all-reduce(bf16[128,128]{1,0:T(8,128)(2,1)S(1)} %convolution_convert_fusion.2), channel_id=1, replica_groups=mesh['elec'=16,'tm'=32] {'elec'}, use_global_device_ids=true, to_apply=%region_9.0 | all-reduce | flops 16384 | bytes 65536 | tf_op jit(solution)/shard_map/psum | solution.py:83
  817.1 3.7 fusion.1
  823.9 76.8 %psum.78 = bf16[128,128]{1,0:T(8,128)(2,1)S(1)} all-reduce(bf16[128,128]{1,0:T(8,128)(2,1)S(1)} %convolution_convert_fusion.1), channel_id=1, replica_groups=mesh['elec'=16,'tm'=32] {'elec'}, use_global_device_ids=true, to_apply=%region_10.0 | all-reduce | flops 16384 | bytes 65536 | tf_op jit(solution)/shard_map/psum | solution.py:83
  900.7 3.6 fusion
  904.3 1.8 convolution_convert_fusion
  906.1 76.8 %psum.79 = bf16[128,128]{1,0:T(8,128)(2,1)S(1)} all-reduce(bf16[128,128]{1,0:T(8,128)(2,1)S(1)} %convolution_convert_fusion), channel_id=1, replica_groups=mesh['elec'=16,'tm'=32] {'elec'}, use_global_device_ids=true, to_apply=%region_11.0 | all-reduce | flops 16384 | bytes 65536 | tf_op jit(solution)/shard_map/psum | solution.py:83
  (74 shorter events, 37.6 us)
Async XLA Ops:
  7.2 183.2 %all-reduce.3.cloned.1.call-start = ((), (), s32[]{:S(2)}) async-start(), calls=%async_computation | async-start | bytes 393216 | tf_op jit(solution)/shard_map/psum | solution.py:60
  8.1 12.2 %collective-permute-start = (bf16[256,16]{1,0:T(8,128)(2,1)S(1)}, bf16[256,16]{1,0:T(8,128)(2,1)S(1)}, u32[]{:S(2)}, u32[]{:S(2)}) collective-permute-start(bf16[256,16]{1,0:T(8,128)(2,1)S(1)} %slice.115), channel_id=1, source_target_pairs={{0,1},{1,2},{2,3},{3,4},{4,5},{5,6},{6,7},{7,8},{8,9},{9,10},{10,1... | collective-permute-start | bytes 24584 | tf_op jit(solution)/shard_map/ppermute | solution.py:18
  14.0 6.4 copy-start
  25.9 416.5 %all-reduce.5.cloned.1.call-start = ((), (), s32[]{:S(2)}) async-start(), calls=%async_computation.1 | async-start | bytes 4194304 | tf_op jit(solution)/shard_map/psum | solution.py:76
  211.3 231.1 %copy-start.4 = (bf16[128,4096]{1,0:T(8,128)(2,1)S(1)}, bf16[128,4096]{1,0:T(8,128)(2,1)}, u32[]{:S(2)}) copy-start(bf16[128,4096]{1,0:T(8,128)(2,1)} %param.3) | copy-start | bytes 3145732
  442.4 49.4 %copy-start.5 = (f32[128,4096]{1,0:T(8,128)S(1)}, f32[128,4096]{1,0:T(8,128)}, u32[]{:S(2)}) copy-start(f32[128,4096]{1,0:T(8,128)} %all-reduce.5.cloned.1.call-done) | copy-start | bytes 6291460
  573.3 1.4 copy-start.3
  737.2 1.4 copy-start.1
  820.8 1.4 copy-start.2
Sparse Core Ops, SparseCore 0:
  26.0 164.3 all-reduce.2
  211.4 230.9 all-reduce.4
where the time goes:
time: 992 us
  blocking collectives  560 us (56%)
  waiting for transfers between devices  346 us (35%)
  matrix products  47.6 us (5%)
  between operations  15.2 us (2%)
  local copies, waits for them, and re-layouts  14.8 us (1%)
    psum x6, blocking collectives, gram_elec(): return lax.psum(value.astype(jnp.bfloat16), 'elec').astype(jnp.float32)  461 us
    psum x1, waiting for transfers between devices, shards(): reduced = lax.psum(gradient_term, 'tm')  177 us
    psum x1, waiting for transfers between devices, shards(): source_sums = lax.psum(partial_sums, 'elec')  164 us
    psum x1, blocking collectives, shards(): deriv_mean = lax.psum(deriv_local, 'tm') / samples_total  53.7 us
    psum x1, blocking collectives, norm_elec(): return lax.psum(value, 'elec')  45.7 us
  transfers between devices with their start and end apart: 3, of which 3 were waited for; matrix products, arithmetic and copies ran while one was open for 1% of the time, Pallas kernels for 0%

commit v1 on v0

v1 whole, which is shorter than its diff:
```python
import functools
import itertools
import math

import jax
import jax.numpy as jnp
from jax import lax
from jax.experimental import pallas as pl
from jax.experimental.pallas import tpu as pltpu
from jax.sharding import PartitionSpec as P

LAGS = 16
NS_STEPS = 6
START = 0.15
MESH = pl.DeviceIdType.MESH
SIZE = dict(x=4, h=4, l=2, z=8, c=2)
F32, BF16 = jnp.float32, jnp.bfloat16
LANES = 128


def hops(move):
    x, y, z = move.get("x", 0), 2 * move.get("h", 0) + move.get("l", 0), move.get("z", 0)
    return min(x, 4 - x) + min(y, 8 - y) + min(z, 8 - z)


def moves(*names):
    every = itertools.product(*[range(SIZE[name]) for name in names])
    found = [dict(zip(names, move)) for move in every if any(move)]
    return sorted(found, key=lambda move: -hops(move))


ELEC, PART, RING = moves("x", "h"), moves("l", "c"), moves("z")


def place():
    elec, tm = lax.axis_index("elec"), lax.axis_index("tm")
    return dict(x=elec // 4, h=elec % 4, l=tm // 16, z=(tm // 2) % 8, c=tm % 2)


def moved(at, move):
    return {k: lax.rem(v + move.get(k, 0), SIZE[k]) for k, v in at.items()}


def elec_of(at):
    return at["x"] * 4 + at["h"]


def tm_of(at):
    return (at["l"] * 8 + at["z"]) * 2 + at["c"]


def part_of(at):
    return at["l"] * 2 + at["c"]


def device(at):
    return {"elec": elec_of(at), "tm": tm_of(at)}


def send(src, dst, sems, slot, at):
    copy = pltpu.make_async_remote_copy(
        src_ref=src,
        dst_ref=dst,
        send_sem=sems[0].at[slot],
        recv_sem=sems[1].at[slot],
        device_id=device(at),
        device_id_type=MESH,
    )
    copy.start()
    return copy


def halves(a):
    top = a.astype(BF16)
    return top, (a - top.astype(F32)).astype(BF16)


def dot(a, b, dims=(((1,), (0,)), ((), ()))):
    return lax.dot_general(a, b, dims, preferred_element_type=F32)


def fine_dot(a, b):
    (a1, a2), (b1, b2) = halves(a), halves(b)
    return dot(jnp.concatenate([a1, a1, a2], 1), jnp.concatenate([b1, b2, b1], 0))


def fine_gram(a):
    a1, a2 = halves(a)
    both = (((1,), (1,)), ((), ()))
    return dot(jnp.concatenate([a1, a1, a2], 1), jnp.concatenate([a1, a2, a1], 1), both)


def lagged(rows):
    turned = [
        pltpu.roll(jnp.broadcast_to(row, (LAGS, LANES)), 0, 1, stride=1, stride_axis=0) for row in rows
    ]
    lane = lax.broadcasted_iota(jnp.int32, (LAGS, LANES), 1)
    late = lax.broadcasted_iota(jnp.int32, (LAGS, LANES), 0)
    return [jnp.where(lane < late, a, b) for a, b in zip(turned, turned[1:])]


def kernel(
    sig, vec, sources, unmixing,
    tail, padded, ext, far_out, far_in, feat, partial, summed, sums, cubes, deriv_out, deriv_in,
    grad_out, grad_in, gram, gram_part, gram_ring, gram_ring_in, gram_elec, gram_elec_in, gram_all,
    tail_s, tail_r, far_s, far_r, rs_s, rs_r, ag_s, ag_r, cube_s, cube_r, deriv_s, deriv_r,
    grad_s, grad_r, g1_s, g1_r, g2_s, g2_r, g3_s, g3_r, g4_s, g4_r,
):
    at = place()
    elec, tm = elec_of(at), tm_of(at)
    length = sig.shape[1]
    tiles = length // LANES
    after, before = lax.rem(tm + 1, 32), lax.rem(tm + 31, 32)

    barrier = pltpu.get_barrier_semaphore()
    for move in ELEC + PART + RING:
        pl.semaphore_signal(barrier, inc=1, device_id=device(moved(at, move)), device_id_type=MESH)
    for other in (after, before):
        pl.semaphore_signal(barrier, inc=1, device_id={"elec": elec, "tm": other}, device_id_type=MESH)
    pl.semaphore_wait(barrier, len(ELEC) + len(PART) + len(RING) + 2)

    tail_copy = pltpu.make_async_remote_copy(
        src_ref=sig.at[:, pl.ds(length - LANES, LANES)],
        dst_ref=tail,
        send_sem=tail_s.at[0],
        recv_sem=tail_r.at[0],
        device_id={"elec": elec, "tm": after},
        device_id_type=MESH,
    )
    tail_copy.start()
    padded[:, LANES:] = sig[...].astype(F32)

    @pl.loop(0, 32)
    def _(block):
        rows = padded[pl.ds(block * 8, 8), LANES:]
        for r in range(8):
            pieces = lagged([rows[r : r + 1, k * LANES : (k + 1) * LANES] for k in range(tiles)])
            for k, piece in enumerate(pieces):
                ext[pl.ds((block * 8 + r) * LAGS, LAGS), (k + 1) * LANES : (k + 2) * LANES] = piece.astype(BF16)

    partial[:, LANES:] = dot(vec[...], ext[:, LANES:])

    tail_copy.wait()
    first = jnp.where(tm > 0, 1.0, 0.0)
    padded[:, :LANES] = tail[...].astype(F32) * first

    @pl.loop(0, 32)
    def _(block):
        rows = padded[pl.ds(block * 8, 8), : 2 * LANES]
        for r in range(8):
            (piece,) = lagged([rows[r : r + 1, :LANES], rows[r : r + 1, LANES:]])
            ext[pl.ds((block * 8 + r) * LAGS, LAGS), :LANES] = piece.astype(BF16)

    far_copies = []
    for i, move in enumerate(PART):
        to = moved(at, move)
        blocks = [pl.multiple_of((to["l"] * 16 + z * 2 + to["c"]) * 8, 8) for z in range(8)]
        far_out[i] = jnp.concatenate([padded[pl.ds(block, 8), :] for block in blocks], 0).astype(BF16)
        far_copies.append(send(far_out.at[i], far_in.at[i], (far_s, far_r), i, to))

    partial[:, :LANES] = dot(vec[...], ext[:, :LANES])

    rs_copies = []
    for i, move in enumerate(ELEC):
        to = moved(at, move)
        rows = pl.ds(pl.multiple_of(elec_of(to) * 8, 8), 8)
        rs_copies.append(send(partial.at[rows], summed.at[i], (rs_s, rs_r), i, to))

    for z in range(8):
        own = pl.multiple_of((at["l"] * 16 + z * 2 + at["c"]) * LANES, LANES)
        feat[z * LANES : (z + 1) * LANES, :length] = ext[pl.ds(own, LANES), :]
    for i, copy in enumerate(far_copies):
        copy.wait()

        @pl.loop(0, 4)
        def _(block):
            rows = far_in[i, pl.ds(block * 16, 16), :].astype(F32)
            for r in range(16):
                pieces = lagged([rows[r : r + 1, k * LANES : (k + 1) * LANES] for k in range(tiles + 1)])
                for k, piece in enumerate(pieces):
                    begin = (i + 1) * length + k * LANES
                    feat[pl.ds((block * 16 + r) * LAGS, LAGS), begin : begin + LANES] = piece.astype(BF16)

    mine = pl.ds(pl.multiple_of(elec * 8, 8), 8)
    total = partial[mine, :]
    for i, copy in enumerate(rs_copies):
        copy.wait()
        total = total + summed[i]
    sums[mine, :] = total
    ag_copies = [
        send(sums.at[mine], sums.at[mine], (ag_s, ag_r), i, moved(at, move)) for i, move in enumerate(ELEC)
    ]
    for copy in ag_copies:
        copy.wait()

    s = sums[...]
    sources[...] = s.astype(BF16)
    cubes[0] = (s * s * s).astype(BF16)
    square = 3.0 * s * s
    deriv = jnp.sum(square, axis=1, keepdims=True)
    deriv_out[...] = jnp.transpose(jnp.broadcast_to(deriv, (LANES, LANES)))[:8]
    cube_copies, deriv_copies = [], []
    for i, move in enumerate(PART):
        to = moved(at, move)
        cube_copies.append(send(cubes.at[0], cubes.at[i + 1], (cube_s, cube_r), i, to))
        deriv_copies.append(send(deriv_out, deriv_in.at[i], (deriv_s, deriv_r), i, to))
    for copy in cube_copies + deriv_copies:
        copy.wait()
    deriv_row = deriv_out[...]
    for i in range(len(PART)):
        deriv_row = deriv_row + deriv_in[i]
    deriv = jnp.transpose(jnp.broadcast_to(deriv_row[:1], (LANES, LANES)))

    cubed = jnp.concatenate([cubes[i] for i in range(len(PART) + 1)], 1)

    def block_of(z):
        rows = pl.ds(pl.multiple_of(z * LANES, LANES), LANES)
        columns = pl.ds(pl.multiple_of((at["l"] * 16 + z * 2 + at["c"]) * LANES, LANES), LANES)
        grad = dot(cubed, feat[rows, :], (((1,), (1,)), ((), ())))
        return grad - deriv * vec[:, columns].astype(F32)

    grad_copies = []
    for i, move in enumerate(RING):
        to = moved(at, move)
        grad_out[i] = block_of(to["z"]).astype(BF16)
        grad_copies.append(send(grad_out.at[i], grad_in.at[i], (grad_s, grad_r), i, to))
    updated = block_of(at["z"])
    for i, copy in enumerate(grad_copies):
        copy.wait()
        updated = updated + grad_in[i].astype(F32)
    updated = updated * (1.0 / (length * 32))

    gram[...] = fine_gram(updated)
    part = part_of(at)
    quarter = pl.ds(pl.multiple_of(part * 32, 32), 32)
    copies = []
    for i, move in enumerate(PART):
        to = moved(at, move)
        rows = pl.ds(pl.multiple_of(part_of(to) * 32, 32), 32)
        copies.append(send(gram.at[rows], gram_part.at[i], (g1_s, g1_r), i, to))
    total = gram[quarter, :]
    for i, copy in enumerate(copies):
        copy.wait()
        total = total + gram_part[i]
    gram_ring[...] = total.astype(BF16)
    copies = [
        send(gram_ring, gram_ring_in.at[i], (g2_s, g2_r), i, moved(at, move)) for i, move in enumerate(RING)
    ]
    total = gram_ring[...].astype(F32)
    for i, copy in enumerate(copies):
        copy.wait()
        total = total + gram_ring_in[i].astype(F32)
    gram_elec[...] = total.astype(BF16)
    copies = [
        send(gram_elec, gram_elec_in.at[i], (g3_s, g3_r), i, moved(at, move)) for i, move in enumerate(ELEC)
    ]
    total = gram_elec[...].astype(F32)
    for i, copy in enumerate(copies):
        copy.wait()
        total = total + gram_elec_in[i].astype(F32)
    gram_all[quarter, :] = total
    copies = [
        send(gram_all.at[quarter], gram_all.at[quarter], (g4_s, g4_r), i, moved(at, move))
        for i, move in enumerate(PART)
    ]
    for copy in copies:
        copy.wait()

    g = gram_all[...]
    row = lax.broadcasted_iota(jnp.int32, (LANES, LANES), 0)
    column = lax.broadcasted_iota(jnp.int32, (LANES, LANES), 1)
    unit = jnp.where(row == column, 1.0, 0.0)
    squares = jnp.sum(jnp.sum(g * unit, axis=1, keepdims=True), axis=0, keepdims=True)
    scale = START * math.sqrt(LANES) * lax.rsqrt(squares + 1e-06)
    g = g * scale * scale
    product = None
    for step in range(NS_STEPS):
        factor = 1.5 * unit - 0.5 * g
        product = factor if product is None else fine_dot(factor, product)
        if step < NS_STEPS - 1:
            g = fine_dot(fine_dot(factor, g), factor)
    unmixing[...] = fine_dot(product, updated * scale)


def sem_pairs(*counts):
    return [pltpu.SemaphoreType.DMA((count,)) for count in counts for _ in range(2)]


def shards(signals, vectors):
    channels, length = signals.shape
    count, columns = vectors.shape
    near, ring, part = len(ELEC), len(RING), len(PART)
    vmem = pl.BlockSpec(memory_space=pltpu.VMEM)
    return pl.pallas_call(
        kernel,
        out_shape=(
            jax.ShapeDtypeStruct((count, length), BF16),
            jax.ShapeDtypeStruct((count, LANES), F32),
        ),
        in_specs=[vmem, vmem],
        out_specs=(vmem, vmem),
        scratch_shapes=[
            pltpu.VMEM((channels, LANES), BF16),
            pltpu.VMEM((channels, LANES + length), F32),
            pltpu.VMEM((columns, length), BF16),
            pltpu.VMEM((part, 64, LANES + length), BF16),
            pltpu.VMEM((part, 64, LANES + length), BF16),
            pltpu.VMEM((8 * LANES, (part + 1) * length), BF16),
            pltpu.VMEM((count, length), F32),
            pltpu.VMEM((near, 8, length), F32),
            pltpu.VMEM((count, length), F32),
            pltpu.VMEM((part + 1, count, length), BF16),
            pltpu.VMEM((8, LANES), F32),
            pltpu.VMEM((part, 8, LANES), F32),
            pltpu.VMEM((ring, count, LANES), BF16),
            pltpu.VMEM((ring, count, LANES), BF16),
            pltpu.VMEM((LANES, LANES), F32),
            pltpu.VMEM((part, 32, LANES), F32),
            pltpu.VMEM((32, LANES), BF16),
            pltpu.VMEM((ring, 32, LANES), BF16),
            pltpu.VMEM((32, LANES), BF16),
            pltpu.VMEM((near, 32, LANES), BF16),
            pltpu.VMEM((LANES, LANES), F32),
            *sem_pairs(1, part, near, near, part, part, ring, part, ring, near, part),
        ],
        compiler_params=pltpu.CompilerParams(
            collective_id=0, has_side_effects=True, vmem_limit_bytes=40 * 2**20
        ),
        cost_estimate=pl.CostEstimate(flops=10**9, bytes_accessed=2 * 10**6, transcendentals=0),
        name="separate",
    )(signals, vectors)


def solution(mesh):
    return jax.shard_map(
        shards,
        mesh=mesh,
        in_specs=(P("elec", "tm"), P(None, "elec")),
        out_specs=(P(None, "tm"), P(None, ("elec", "tm"))),
        check_vma=False,
    )
```

time: 992 us -> 76.4 us (0.08)
  the two profiles are of different devices: /device:TPU:8 before, /device:TPU:1 now
where the time goes in v1:
time: 76.4 us; the launch traced here: 76.3 us
  Pallas kernels  72.2 us (95%)
  local copies, waits for them, and re-layouts  3.42 us (4%)
    pallas_call x1, Pallas kernels, shards(): pl.pallas_call(kernel, out_shape=(jax.ShapeDtypeStruct((count, length), B...  72.2 us
    unnamed x6, local copies, waits for them, and re-layouts  3.42 us

profile of v1, /device:TPU:1, one launch (start us, length us, event | category | flops | bytes accessed | tf_op | source)
XLA Modules:
  0.0 76.3 jit_solution(12771174812102502339)
XLA Ops:
  0.6 0.0 copy-start
  0.6 1.2 %copy-done = bf16[128,4096]{1,0:T(8,128)(2,1)S(1)} copy-done((bf16[128,4096]{1,0:T(8,128)(2,1)S(1)}, bf16[128,4096]{1,0:T(8,128)(2,1)}, u32[]{:S(2)}) %copy-start) | copy-done | bytes 1048600
  1.9 0.0 copy-start.1
  1.9 0.9 %copy-done.1 = bf16[256,384]{1,0:T(8,128)(2,1)S(1)} copy-done((bf16[256,384]{1,0:T(8,128)(2,1)S(1)}, bf16[256,384]{1,0:T(8,128)(2,1)}, u32[]{:S(2)}) %copy-start.1) | copy-done | bytes 196632
  2.8 72.2 %separate.1 = (bf16[128,384]{1,0:T(8,128)(2,1)S(1)}, f32[128,128]{1,0:T(8,128)S(1)}) custom-call(bf16[256,384]{1,0:T(8,128)(2,1)S(1)} %copy-done.1, bf16[128,4096]{1,0:T(8,128)(2,1)S(1)} %copy-done), custom_call_target="tpu_custom_call" | custom-call | flops 1000000000 | bytes 2000000 | tf_op jit(solution)/shard_map/separate/pallas_call | solution.py:294
  75.0 0.6 copy.6
  75.6 0.6 copy.7
Async XLA Ops:
  0.6 1.2 %copy-start = (bf16[128,4096]{1,0:T(8,128)(2,1)S(1)}, bf16[128,4096]{1,0:T(8,128)(2,1)}, u32[]{:S(2)}) copy-start(bf16[128,4096]{1,0:T(8,128)(2,1)} %vec.1) | copy-start | bytes 3145732
  1.9 0.9 %copy-start.1 = (bf16[256,384]{1,0:T(8,128)(2,1)S(1)}, bf16[256,384]{1,0:T(8,128)(2,1)}, u32[]{:S(2)}) copy-start(bf16[256,384]{1,0:T(8,128)(2,1)} %sig.1) | copy-start | bytes 589828

commit v2 on v1

--- a/solution.py
+++ b/solution.py
@@ -29,7 +29,8 @@
     return sorted(found, key=lambda move: -hops(move))
 
 
-ELEC, PART, RING = moves("x", "h"), moves("l", "c"), moves("z")
+ELEC, PLANE, RING = moves("x", "h"), moves("x", "h", "l"), moves("z")
+PART = [dict(l=1), dict(c=1), dict(l=1, c=1)]
 
 
 def place():
@@ -90,20 +91,15 @@
     return dot(jnp.concatenate([a1, a1, a2], 1), jnp.concatenate([a1, a2, a1], 1), both)
 
 
-def lagged(rows):
-    turned = [
-        pltpu.roll(jnp.broadcast_to(row, (LAGS, LANES)), 0, 1, stride=1, stride_axis=0) for row in rows
-    ]
-    lane = lax.broadcasted_iota(jnp.int32, (LAGS, LANES), 1)
-    late = lax.broadcasted_iota(jnp.int32, (LAGS, LANES), 0)
-    return [jnp.where(lane < late, a, b) for a, b in zip(turned, turned[1:])]
+def lagged(row):
+    return pltpu.roll(jnp.broadcast_to(row, (LAGS, LANES)), 0, 1, stride=1, stride_axis=0)
 
 
 def kernel(
-    sig, vec, sources, unmixing,
-    tail, padded, ext, far_out, far_in, feat, partial, summed, sums, cubes, deriv_out, deriv_in,
+    sig_hbm, vec_hbm, sources, unmixing,
+    sig, vec, tail, padded, ext, far_out, far_in, feat, partial, summed, blocks, waves, cubes,
     grad_out, grad_in, gram, gram_part, gram_ring, gram_ring_in, gram_elec, gram_elec_in, gram_all,
-    tail_s, tail_r, far_s, far_r, rs_s, rs_r, ag_s, ag_r, cube_s, cube_r, deriv_s, deriv_r,
+    load, tail_s, tail_r, far_s, far_r, rs1_s, rs1_r, rs2_s, rs2_r, cube_s, cube_r, core_s, core_r, wave_s, wave_r,
     grad_s, grad_r, g1_s, g1_r, g2_s, g2_r, g3_s, g3_r, g4_s, g4_r,
 ):
     at = place()
@@ -112,13 +108,37 @@
     tiles = length // LANES
     after, before = lax.rem(tm + 1, 32), lax.rem(tm + 31, 32)
 
+    loads = [
+        pltpu.make_async_copy(sig_hbm, sig, load.at[0]),
+        pltpu.make_async_copy(vec_hbm, vec, load.at[1]),
+    ]
+    for copy in loads:
+        copy.start()
     barrier = pltpu.get_barrier_semaphore()
-    for move in ELEC + PART + RING:
-        pl.semaphore_signal(barrier, inc=1, device_id=device(moved(at, move)), device_id_type=MESH)
     for other in (after, before):
         pl.semaphore_signal(barrier, inc=1, device_id={"elec": elec, "tm": other}, device_id_type=MESH)
-    pl.semaphore_wait(barrier, len(ELEC) + len(PART) + len(RING) + 2)
-
+    greeted = PLANE + RING + PART[1:]
+    for move in greeted:
+        pl.semaphore_signal(barrier, inc=1, device_id=device(moved(at, move)), device_id_type=MESH)
+
+    lane = lax.broadcasted_iota(jnp.int32, (LAGS, LANES), 1)
+    late = lax.broadcasted_iota(jnp.int32, (LAGS, LANES), 0)
+    spill = lane < late
+
+    loads[0].wait()
+    padded[:, LANES:] = sig[...].astype(F32)
+
+    @pl.loop(0, 16)
+    def _(block):
+        rows = padded[pl.ds(block * 16, 16), LANES:]
+        for r in range(16):
+            to = pl.ds((block * 16 + r) * LAGS, LAGS)
+            turned = [lagged(rows[r : r + 1, k * LANES : (k + 1) * LANES]) for k in range(tiles)]
+            ext[to, :LANES] = turned[0].astype(BF16)
+            for k in range(1, tiles):
+                ext[to, k * LANES : (k + 1) * LANES] = jnp.where(spill, turned[k - 1], turned[k]).astype(BF16)
+
+    pl.semaphore_wait(barrier, len(greeted) + 2)
     tail_copy = pltpu.make_async_remote_copy(
         src_ref=sig.at[:, pl.ds(length - LANES, LANES)],
         dst_ref=tail,
@@ -128,47 +148,72 @@
         device_id_type=MESH,
     )
     tail_copy.start()
-    padded[:, LANES:] = sig[...].astype(F32)
-
-    @pl.loop(0, 32)
-    def _(block):
-        rows = padded[pl.ds(block * 8, 8), LANES:]
-        for r in range(8):
-            pieces = lagged([rows[r : r + 1, k * LANES : (k + 1) * LANES] for k in range(tiles)])
-            for k, piece in enumerate(pieces):
-                ext[pl.ds((block * 8 + r) * LAGS, LAGS), (k + 1) * LANES : (k + 2) * LANES] = piece.astype(BF16)
-
+    loads[1].wait()
     partial[:, LANES:] = dot(vec[...], ext[:, LANES:])
+    rs_copies = []
+    for i, move in enumerate(ELEC):
+        to = moved(at, move)
+        rows = pl.ds(pl.multiple_of(elec_of(to) * 8, 8), 8)
+        rs_copies.append(
+            send(partial.at[rows, pl.ds(LANES, length - LANES)], summed.at[i, :, pl.ds(LANES, length - LANES)], (rs1_s, rs1_r), i, to)
+        )
 
     tail_copy.wait()
     first = jnp.where(tm > 0, 1.0, 0.0)
     padded[:, :LANES] = tail[...].astype(F32) * first
 
-    @pl.loop(0, 32)
+    @pl.loop(0, 8)
     def _(block):
-        rows = padded[pl.ds(block * 8, 8), : 2 * LANES]
-        for r in range(8):
-            (piece,) = lagged([rows[r : r + 1, :LANES], rows[r : r + 1, LANES:]])
-            ext[pl.ds((block * 8 + r) * LAGS, LAGS), :LANES] = piece.astype(BF16)
+        rows = padded[pl.ds(block * 32, 32), :LANES]
+        for r in range(32):
+            to = pl.ds((block * 32 + r) * LAGS, LAGS)
+            ext[to, :LANES] = jnp.where(spill, lagged(rows[r : r + 1]), ext[to, :LANES].astype(F32)).astype(BF16)
+
+    partial[:, :LANES] = dot(vec[...], ext[:, :LANES])
+    for i, move in enumerate(ELEC):
+        to = moved(at, move)
+        rows = pl.ds(pl.multiple_of(elec_of(to) * 8, 8), 8)
+        rs_copies.append(
+            send(partial.at[rows, pl.ds(0, LANES)], summed.at[i, :, pl.ds(0, LANES)], (rs2_s, rs2_r), i, to)
+        )
 
     far_copies = []
     for i, move in enumerate(PART):
         to = moved(at, move)
-        blocks = [pl.multiple_of((to["l"] * 16 + z * 2 + to["c"]) * 8, 8) for z in range(8)]
-        far_out[i] = jnp.concatenate([padded[pl.ds(block, 8), :] for block in blocks], 0).astype(BF16)
+        starts = [pl.multiple_of((to["l"] * 16 + z * 2 + to["c"]) * 8, 8) for z in range(8)]
+        far_out[i] = jnp.concatenate([padded[pl.ds(start, 8), :] for start in starts], 0).astype(BF16)
         far_copies.append(send(far_out.at[i], far_in.at[i], (far_s, far_r), i, to))
-
-    partial[:, :LANES] = dot(vec[...], ext[:, :LANES])
-
-    rs_copies = []
-    for i, move in enumerate(ELEC):
-        to = moved(at, move)
-        rows = pl.ds(pl.multiple_of(elec_of(to) * 8, 8), 8)
-        rs_copies.append(send(partial.at[rows], summed.at[i], (rs_s, rs_r), i, to))
-
     for z in range(8):
         own = pl.multiple_of((at["l"] * 16 + z * 2 + at["c"]) * LANES, LANES)
         feat[z * LANES : (z + 1) * LANES, :length] = ext[pl.ds(own, LANES), :]
+
+    mine = pl.ds(pl.multiple_of(elec * 8, 8), 8)
+    total = partial[mine, :]
+    for copy in rs_copies:
+        copy.wait()
+    for i in range(len(ELEC)):
+        total = total + summed[i]
+
+    def stacked(block, last):
+        return jnp.concatenate([block[:, k * LANES : (k + 1) * LANES] for k in range(tiles)] + [last], 0).astype(BF16)
+
+    deriv = jnp.sum(3.0 * total * total, axis=1, keepdims=True)
+    high = deriv.astype(BF16).astype(F32)
+    middle = (deriv - high).astype(BF16).astype(F32)
+    low = deriv - high - middle
+    lane = lax.broadcasted_iota(jnp.int32, (8, LANES), 1)
+    pad = jnp.where(lane == 0, high, jnp.where(lane == 1, middle, jnp.where(lane == 2, low, 0.0)))
+    blocks[0, elec] = stacked(total * total * total, pad)
+    waves[elec] = stacked(total, jnp.zeros((8, LANES), F32))
+    cube_copies = []
+    for i, move in enumerate(PLANE):
+        cube_copies.append(
+            send(blocks.at[0, elec], blocks.at[move["l"], elec], (cube_s, cube_r), i, moved(at, move))
+        )
+    wave_copies = [
+        send(waves.at[elec], waves.at[elec], (wave_s, wave_r), i, moved(at, move)) for i, move in enumerate(ELEC)
+    ]
+
     for i, copy in enumerate(far_copies):
         copy.wait()
 
@@ -176,47 +221,36 @@
         def _(block):
             rows = far_in[i, pl.ds(block * 16, 16), :].astype(F32)
             for r in range(16):
-                pieces = lagged([rows[r : r + 1, k * LANES : (k + 1) * LANES] for k in range(tiles + 1)])
-                for k, piece in enumerate(pieces):
+                to = pl.ds((block * 16 + r) * LAGS, LAGS)
+                turned = [lagged(rows[r : r + 1, k * LANES : (k + 1) * LANES]) for k in range(tiles + 1)]
+                for k in range(tiles):
                     begin = (i + 1) * length + k * LANES
-                    feat[pl.ds((block * 16 + r) * LAGS, LAGS), begin : begin + LANES] = piece.astype(BF16)
-
-    mine = pl.ds(pl.multiple_of(elec * 8, 8), 8)
-    total = partial[mine, :]
-    for i, copy in enumerate(rs_copies):
-        copy.wait()
-        total = total + summed[i]
-    sums[mine, :] = total
-    ag_copies = [
-        send(sums.at[mine], sums.at[mine], (ag_s, ag_r), i, moved(at, move)) for i, move in enumerate(ELEC)
-    ]
-    for copy in ag_copies:
-        copy.wait()
-
-    s = sums[...]
-    sources[...] = s.astype(BF16)
-    cubes[0] = (s * s * s).astype(BF16)
-    square = 3.0 * s * s
-    deriv = jnp.sum(square, axis=1, keepdims=True)
-    deriv_out[...] = jnp.transpose(jnp.broadcast_to(deriv, (LANES, LANES)))[:8]
-    cube_copies, deriv_copies = [], []
-    for i, move in enumerate(PART):
-        to = moved(at, move)
-        cube_copies.append(send(cubes.at[0], cubes.at[i + 1], (cube_s, cube_r), i, to))
-        deriv_copies.append(send(deriv_out, deriv_in.at[i], (deriv_s, deriv_r), i, to))
-    for copy in cube_copies + deriv_copies:
-        copy.wait()
-    deriv_row = deriv_out[...]
-    for i in range(len(PART)):
-        deriv_row = deriv_row + deriv_in[i]
-    deriv = jnp.transpose(jnp.broadcast_to(deriv_row[:1], (LANES, LANES)))
-
-    cubed = jnp.concatenate([cubes[i] for i in range(len(PART) + 1)], 1)
+                    feat[to, begin : begin + LANES] = jnp.where(spill, turned[k], turned[k + 1]).astype(BF16)
+
+    for copy in cube_copies:
+        copy.wait()
+    core_copy = send(blocks.at[pl.ds(0, 2)], blocks.at[pl.ds(2, 2)], (core_s, core_r), 0, moved(at, PART[1]))
+
+    def unpack(shard):
+        pads = []
+        for pair in range(8):
+            pieces = [blocks[shard, 2 * pair + k].astype(F32) for k in range(2)]
+            for k in range(tiles):
+                rows = jnp.concatenate([piece[8 * k : 8 * k + 8] for piece in pieces], 0)
+                begin = shard * length + k * LANES
+                cubes[16 * pair : 16 * pair + 16, begin : begin + LANES] = rows.astype(BF16)
+            pads += [piece[8 * tiles :] for piece in pieces]
+        return jnp.concatenate(pads, 0)
+
+    pads = unpack(0) + unpack(1)
+    core_copy.wait()
+    pads = pads + unpack(2) + unpack(3)
+    deriv = jnp.sum(pads, axis=1, keepdims=True)
 
     def block_of(z):
         rows = pl.ds(pl.multiple_of(z * LANES, LANES), LANES)
         columns = pl.ds(pl.multiple_of((at["l"] * 16 + z * 2 + at["c"]) * LANES, LANES), LANES)
-        grad = dot(cubed, feat[rows, :], (((1,), (1,)), ((), ())))
+        grad = dot(cubes[...], feat[rows, :], (((1,), (1,)), ((), ())))
         return grad - deriv * vec[:, columns].astype(F32)
 
     grad_copies = []
@@ -225,6 +259,13 @@
         grad_out[i] = block_of(to["z"]).astype(BF16)
         grad_copies.append(send(grad_out.at[i], grad_in.at[i], (grad_s, grad_r), i, to))
     updated = block_of(at["z"])
+    for copy in wave_copies:
+        copy.wait()
+    for pair in range(8):
+        pieces = [waves[2 * pair + k].astype(F32) for k in range(2)]
+        for k in range(tiles):
+            rows = jnp.concatenate([piece[8 * k : 8 * k + 8] for piece in pieces], 0)
+            sources[16 * pair : 16 * pair + 16, k * LANES : (k + 1) * LANES] = rows.astype(BF16)
     for i, copy in enumerate(grad_copies):
         copy.wait()
         updated = updated + grad_in[i].astype(F32)
@@ -289,7 +330,7 @@
 def shards(signals, vectors):
     channels, length = signals.shape
     count, columns = vectors.shape
-    near, ring, part = len(ELEC), len(RING), len(PART)
+    near, plane, ring, part = len(ELEC), len(PLANE), len(RING), len(PART)
     vmem = pl.BlockSpec(memory_space=pltpu.VMEM)
     return pl.pallas_call(
         kernel,
@@ -297,9 +338,11 @@
             jax.ShapeDtypeStruct((count, length), BF16),
             jax.ShapeDtypeStruct((count, LANES), F32),
         ),
-        in_specs=[vmem, vmem],
+        in_specs=[pl.BlockSpec(memory_space=pltpu.HBM)] * 2,
         out_specs=(vmem, vmem),
         scratch_shapes=[
+            pltpu.VMEM((channels, length), BF16),
+            pltpu.VMEM((count, columns), BF16),
             pltpu.VMEM((channels, LANES), BF16),
             pltpu.VMEM((channels, LANES + length), F32),
             pltpu.VMEM((columns, length), BF16),
@@ -308,10 +351,9 @@
             pltpu.VMEM((8 * LANES, (part + 1) * length), BF16),
             pltpu.VMEM((count, length), F32),
             pltpu.VMEM((near, 8, length), F32),
-            pltpu.VMEM((count, length), F32),
-            pltpu.VMEM((part + 1, count, length), BF16),
-            pltpu.VMEM((8, LANES), F32),
-            pltpu.VMEM((part, 8, LANES), F32),
+            pltpu.VMEM((part + 1, near + 1, 32, LANES), BF16),
+            pltpu.VMEM((near + 1, 32, LANES), BF16),
+            pltpu.VMEM((count, (part + 1) * length), BF16),
             pltpu.VMEM((ring, count, LANES), BF16),
             pltpu.VMEM((ring, count, LANES), BF16),
             pltpu.VMEM((LANES, LANES), F32),
@@ -321,14 +363,15 @@
             pltpu.VMEM((32, LANES), BF16),
             pltpu.VMEM((near, 32, LANES), BF16),
             pltpu.VMEM((LANES, LANES), F32),
-            *sem_pairs(1, part, near, near, part, part, ring, part, ring, near, part),
+            pltpu.SemaphoreType.DMA((2,)),
+            *sem_pairs(1, part, near, near, plane, 1, near, ring, part, ring, near, part),
         ],
         compiler_params=pltpu.CompilerParams(
             collective_id=0, has_side_effects=True, vmem_limit_bytes=40 * 2**20
         ),
         cost_estimate=pl.CostEstimate(flops=10**9, bytes_accessed=2 * 10**6, transcendentals=0),
         name="separate",
-    )(signals, vectors)
+    )(*[pltpu.with_memory_space_constraint(a, pltpu.HBM) for a in (signals, vectors)])
 
 
 def solution(mesh):

time: 76.4 us -> 67.7 us (0.89)
  Pallas kernels: 72.2 us -> 65.7 us
  local copies, waits for them, and re-layouts: 3.42 us -> 1.27 us
    pallas_call x1, Pallas kernels: 72.2 us -> 65.7 us  [shards(): pl.pallas_call(kernel, out_shape=(jax.ShapeDtypeStruct((count, length), B...]
    unnamed x6 -> x2, local copies, waits for them, and re-layouts: 3.42 us -> 1.27 us
where the time goes in v2:
time: 67.7 us; the launch traced here: 67.6 us
  Pallas kernels  65.7 us (97%)
  local copies, waits for them, and re-layouts  1.27 us (2%)
    pallas_call x1, Pallas kernels, shards(): pl.pallas_call(kernel, out_shape=(jax.ShapeDtypeStruct((count, length), B...  65.7 us

profile of v2, /device:TPU:1, one launch (start us, length us, event | category | flops | bytes accessed | tf_op | source)
XLA Modules:
  0.0 67.6 jit_solution(2580454436133281582)
XLA Ops:
  0.6 65.7 %separate.1 = (bf16[128,384]{1,0:T(8,128)(2,1)S(1)}, f32[128,128]{1,0:T(8,128)S(1)}) custom-call(bf16[256,384]{1,0:T(8,128)(2,1)} %sig_hbm.1, bf16[128,4096]{1,0:T(8,128)(2,1)} %vec_hbm.1), custom_call_target="tpu_custom_call" | custom-call | flops 1000000000 | bytes 2000000 | tf_op jit(solution)/shard_map/separate/pallas_call | solution.py:335
  66.3 0.6 copy.6
  67.0 0.6 copy.7

commit v3 on v2

--- a/solution.py
+++ b/solution.py
@@ -31,6 +31,12 @@
 
 ELEC, PLANE, RING = moves("x", "h"), moves("x", "h", "l"), moves("z")
 PART = [dict(l=1), dict(c=1), dict(l=1, c=1)]
+BRICK, SHEET = moves("x", "l", "c"), moves("z", "h")
+
+
+def unique(found):
+    seen = {tuple(move.get(name, 0) for name in SIZE): None for move in found}
+    return [dict(zip(SIZE, move)) for move in seen]
 
 
 def place():
@@ -50,21 +56,21 @@
     return (at["l"] * 8 + at["z"]) * 2 + at["c"]
 
 
-def part_of(at):
-    return at["l"] * 2 + at["c"]
+def brick_of(at):
+    return (at["x"] * 2 + at["l"]) * 2 + at["c"]
 
 
 def device(at):
     return {"elec": elec_of(at), "tm": tm_of(at)}
 
 
-def send(src, dst, sems, slot, at):
+def send(src, dst, sems, slot, to):
     copy = pltpu.make_async_remote_copy(
         src_ref=src,
         dst_ref=dst,
         send_sem=sems[0].at[slot],
         recv_sem=sems[1].at[slot],
-        device_id=device(at),
+        device_id=to,
         device_id_type=MESH,
     )
     copy.start()
@@ -97,10 +103,10 @@
 
 def kernel(
     sig_hbm, vec_hbm, sources, unmixing,
-    sig, vec, tail, padded, ext, far_out, far_in, feat, partial, summed, blocks, waves, cubes,
-    grad_out, grad_in, gram, gram_part, gram_ring, gram_ring_in, gram_elec, gram_elec_in, gram_all,
+    sig, vec, tail, padded, ext, far_out, far_in, feat, partial, summed, spilled, blocks, waves, cubes,
+    half, grad_out, grad_in, gram, gram_brick, gram_sum, gram_sheet, gram_all,
     load, tail_s, tail_r, far_s, far_r, rs1_s, rs1_r, rs2_s, rs2_r, cube_s, cube_r, core_s, core_r, wave_s, wave_r,
-    grad_s, grad_r, g1_s, g1_r, g2_s, g2_r, g3_s, g3_r, g4_s, g4_r,
+    grad_s, grad_r, g1_s, g1_r, g2_s, g2_r, g3_s, g3_r,
 ):
     at = place()
     elec, tm = elec_of(at), tm_of(at)
@@ -114,85 +120,79 @@
     ]
     for copy in loads:
         copy.start()
+    greeted = unique(PLANE + RING + PART + BRICK + SHEET)
     barrier = pltpu.get_barrier_semaphore()
-    for other in (after, before):
-        pl.semaphore_signal(barrier, inc=1, device_id={"elec": elec, "tm": other}, device_id_type=MESH)
-    greeted = PLANE + RING + PART[1:]
     for move in greeted:
         pl.semaphore_signal(barrier, inc=1, device_id=device(moved(at, move)), device_id_type=MESH)
+    for move in ELEC + [{}]:
+        other = {"elec": elec_of(moved(at, move)), "tm": before}
+        pl.semaphore_signal(barrier, inc=1, device_id=other, device_id_type=MESH)
 
     lane = lax.broadcasted_iota(jnp.int32, (LAGS, LANES), 1)
     late = lax.broadcasted_iota(jnp.int32, (LAGS, LANES), 0)
     spill = lane < late
 
     loads[0].wait()
-    padded[:, LANES:] = sig[...].astype(F32)
 
     @pl.loop(0, 16)
     def _(block):
-        rows = padded[pl.ds(block * 16, 16), LANES:]
+        rows = sig[pl.ds(block * 16, 16), :].astype(F32)
         for r in range(16):
             to = pl.ds((block * 16 + r) * LAGS, LAGS)
             turned = [lagged(rows[r : r + 1, k * LANES : (k + 1) * LANES]) for k in range(tiles)]
-            ext[to, :LANES] = turned[0].astype(BF16)
-            for k in range(1, tiles):
-                ext[to, k * LANES : (k + 1) * LANES] = jnp.where(spill, turned[k - 1], turned[k]).astype(BF16)
-
-    pl.semaphore_wait(barrier, len(greeted) + 2)
-    tail_copy = pltpu.make_async_remote_copy(
-        src_ref=sig.at[:, pl.ds(length - LANES, LANES)],
-        dst_ref=tail,
-        send_sem=tail_s.at[0],
-        recv_sem=tail_r.at[0],
-        device_id={"elec": elec, "tm": after},
-        device_id_type=MESH,
-    )
-    tail_copy.start()
+            for k, (a, b) in enumerate(zip([0.0] + turned, turned + [0.0])):
+                ext[to, k * LANES : (k + 1) * LANES] = jnp.where(spill, a, b).astype(BF16)
+
     loads[1].wait()
-    partial[:, LANES:] = dot(vec[...], ext[:, LANES:])
-    rs_copies = []
-    for i, move in enumerate(ELEC):
+    partial[...] = dot(vec[...], ext[...])
+    pl.semaphore_wait(barrier, len(greeted) + len(ELEC) + 1)
+    rs_copies, spill_copies = [], []
+    for i, move in enumerate(ELEC + [{}]):
         to = moved(at, move)
         rows = pl.ds(pl.multiple_of(elec_of(to) * 8, 8), 8)
-        rs_copies.append(
-            send(partial.at[rows, pl.ds(LANES, length - LANES)], summed.at[i, :, pl.ds(LANES, length - LANES)], (rs1_s, rs1_r), i, to)
+        if move:
+            rs_copies.append(send(partial.at[rows, pl.ds(0, length)], summed.at[i], (rs1_s, rs1_r), i, device(to)))
+        over = {"elec": elec_of(to), "tm": after}
+        spill_copies.append(
+            send(partial.at[rows, pl.ds(length, LANES)], spilled.at[i], (rs2_s, rs2_r), i, over)
         )
-
+    tail_copy = send(
+        sig.at[:, pl.ds(length - LANES, LANES)], tail, (tail_s, tail_r), 0, {"elec": elec, "tm": after}
+    )
+
+    padded[:, LANES:] = sig[...].astype(F32)
+    for z in range(8):
+        own = pl.multiple_of((at["l"] * 16 + z * 2 + at["c"]) * LANES, LANES)
+        feat[z * LANES : (z + 1) * LANES, :length] = ext[pl.ds(own, LANES), :length]
     tail_copy.wait()
     first = jnp.where(tm > 0, 1.0, 0.0)
     padded[:, :LANES] = tail[...].astype(F32) * first
-
-    @pl.loop(0, 8)
-    def _(block):
-        rows = padded[pl.ds(block * 32, 32), :LANES]
-        for r in range(32):
-            to = pl.ds((block * 32 + r) * LAGS, LAGS)
-            ext[to, :LANES] = jnp.where(spill, lagged(rows[r : r + 1]), ext[to, :LANES].astype(F32)).astype(BF16)
-
-    partial[:, :LANES] = dot(vec[...], ext[:, :LANES])
-    for i, move in enumerate(ELEC):
-        to = moved(at, move)
-        rows = pl.ds(pl.multiple_of(elec_of(to) * 8, 8), 8)
-        rs_copies.append(
-            send(partial.at[rows, pl.ds(0, LANES)], summed.at[i, :, pl.ds(0, LANES)], (rs2_s, rs2_r), i, to)
-        )
 
     far_copies = []
     for i, move in enumerate(PART):
         to = moved(at, move)
         starts = [pl.multiple_of((to["l"] * 16 + z * 2 + to["c"]) * 8, 8) for z in range(8)]
         far_out[i] = jnp.concatenate([padded[pl.ds(start, 8), :] for start in starts], 0).astype(BF16)
-        far_copies.append(send(far_out.at[i], far_in.at[i], (far_s, far_r), i, to))
-    for z in range(8):
-        own = pl.multiple_of((at["l"] * 16 + z * 2 + at["c"]) * LANES, LANES)
-        feat[z * LANES : (z + 1) * LANES, :length] = ext[pl.ds(own, LANES), :]
+        far_copies.append(send(far_out.at[i], far_in.at[i], (far_s, far_r), i, device(to)))
+
+    @pl.loop(0, 8)
+    def _(z):
+        start = pl.multiple_of((at["l"] * 16 + z * 2 + at["c"]) * 8, 8)
+        rows = padded[pl.ds(start, 8), :LANES]
+        for r in range(8):
+            to = pl.ds((z * 8 + r) * LAGS, LAGS)
+            feat[to, :LANES] = jnp.where(spill, lagged(rows[r : r + 1]), feat[to, :LANES].astype(F32)).astype(BF16)
 
     mine = pl.ds(pl.multiple_of(elec * 8, 8), 8)
-    total = partial[mine, :]
-    for copy in rs_copies:
+    total = partial[mine, :length]
+    for copy in rs_copies + spill_copies:
         copy.wait()
     for i in range(len(ELEC)):
         total = total + summed[i]
+    over = spilled[0]
+    for i in range(len(ELEC)):
+        over = over + spilled[i + 1]
+    total = jnp.concatenate([total[:, :LANES] + over * first, total[:, LANES:]], 1)
 
     def stacked(block, last):
         return jnp.concatenate([block[:, k * LANES : (k + 1) * LANES] for k in range(tiles)] + [last], 0).astype(BF16)
@@ -208,10 +208,11 @@
     cube_copies = []
     for i, move in enumerate(PLANE):
         cube_copies.append(
-            send(blocks.at[0, elec], blocks.at[move["l"], elec], (cube_s, cube_r), i, moved(at, move))
+            send(blocks.at[0, elec], blocks.at[move["l"], elec], (cube_s, cube_r), i, device(moved(at, move)))
         )
     wave_copies = [
-        send(waves.at[elec], waves.at[elec], (wave_s, wave_r), i, moved(at, move)) for i, move in enumerate(ELEC)
+        send(waves.at[elec], waves.at[elec], (wave_s, wave_r), i, device(moved(at, move)))
+        for i, move in enumerate(ELEC)
     ]
 
     for i, copy in enumerate(far_copies):
@@ -229,7 +230,7 @@
 
     for copy in cube_copies:
         copy.wait()
-    core_copy = send(blocks.at[pl.ds(0, 2)], blocks.at[pl.ds(2, 2)], (core_s, core_r), 0, moved(at, PART[1]))
+    core_copy = send(blocks.at[pl.ds(0, 2)], blocks.at[pl.ds(2, 2)], (core_s, core_r), 0, device(moved(at, PART[1])))
 
     def unpack(shard):
         pads = []
@@ -242,7 +243,10 @@
             pads += [piece[8 * tiles :] for piece in pieces]
         return jnp.concatenate(pads, 0)
 
+    both = (((1,), (1,)), ((), ()))
     pads = unpack(0) + unpack(1)
+    for z in range(8):
+        half[z] = dot(cubes[:, : 2 * length], feat[z * LANES : (z + 1) * LANES, : 2 * length], both)
     core_copy.wait()
     pads = pads + unpack(2) + unpack(3)
     deriv = jnp.sum(pads, axis=1, keepdims=True)
@@ -250,14 +254,14 @@
     def block_of(z):
         rows = pl.ds(pl.multiple_of(z * LANES, LANES), LANES)
         columns = pl.ds(pl.multiple_of((at["l"] * 16 + z * 2 + at["c"]) * LANES, LANES), LANES)
-        grad = dot(cubes[...], feat[rows, :], (((1,), (1,)), ((), ())))
+        grad = half[z] + dot(cubes[:, 2 * length :], feat[rows, 2 * length :], both)
         return grad - deriv * vec[:, columns].astype(F32)
 
     grad_copies = []
     for i, move in enumerate(RING):
         to = moved(at, move)
         grad_out[i] = block_of(to["z"]).astype(BF16)
-        grad_copies.append(send(grad_out.at[i], grad_in.at[i], (grad_s, grad_r), i, to))
+        grad_copies.append(send(grad_out.at[i], grad_in.at[i], (grad_s, grad_r), i, device(to)))
     updated = block_of(at["z"])
     for copy in wave_copies:
         copy.wait()
@@ -272,37 +276,29 @@
     updated = updated * (1.0 / (length * 32))
 
     gram[...] = fine_gram(updated)
-    part = part_of(at)
-    quarter = pl.ds(pl.multiple_of(part * 32, 32), 32)
+    mine = pl.ds(pl.multiple_of(brick_of(at) * 8, 8), 8)
     copies = []
-    for i, move in enumerate(PART):
+    for i, move in enumerate(BRICK):
         to = moved(at, move)
-        rows = pl.ds(pl.multiple_of(part_of(to) * 32, 32), 32)
-        copies.append(send(gram.at[rows], gram_part.at[i], (g1_s, g1_r), i, to))
-    total = gram[quarter, :]
-    for i, copy in enumerate(copies):
-        copy.wait()
-        total = total + gram_part[i]
-    gram_ring[...] = total.astype(BF16)
+        rows = pl.ds(pl.multiple_of(brick_of(to) * 8, 8), 8)
+        copies.append(send(gram.at[rows], gram_brick.at[i], (g1_s, g1_r), i, device(to)))
+    total = gram[mine, :]
+    for copy in copies:
+        copy.wait()
+    for i in range(len(BRICK)):
+        total = total + gram_brick[i]
+    gram_sum[...] = total
     copies = [
-        send(gram_ring, gram_ring_in.at[i], (g2_s, g2_r), i, moved(at, move)) for i, move in enumerate(RING)
+        send(gram_sum, gram_sheet.at[i], (g2_s, g2_r), i, device(moved(at, move))) for i, move in enumerate(SHEET)
     ]
-    total = gram_ring[...].astype(F32)
-    for i, copy in enumerate(copies):
-        copy.wait()
-        total = total + gram_ring_in[i].astype(F32)
-    gram_elec[...] = total.astype(BF16)
+    for copy in copies:
+        copy.wait()
+    for i in range(len(SHEET)):
+        total = total + gram_sheet[i]
+    gram_all[mine, :] = total
     copies = [
-        send(gram_elec, gram_elec_in.at[i], (g3_s, g3_r), i, moved(at, move)) for i, move in enumerate(ELEC)
-    ]
-    total = gram_elec[...].astype(F32)
-    for i, copy in enumerate(copies):
-        copy.wait()
-        total = total + gram_elec_in[i].astype(F32)
-    gram_all[quarter, :] = total
-    copies = [
-        send(gram_all.at[quarter], gram_all.at[quarter], (g4_s, g4_r), i, moved(at, move))
-        for i, move in enumerate(PART)
+        send(gram_all.at[mine], gram_all.at[mine], (g3_s, g3_r), i, device(moved(at, move)))
+        for i, move in enumerate(BRICK)
     ]
     for copy in copies:
         copy.wait()
@@ -330,7 +326,7 @@
 def shards(signals, vectors):
     channels, length = signals.shape
     count, columns = vectors.shape
-    near, plane, ring, part = len(ELEC), len(PLANE), len(RING), len(PART)
+    near, plane, ring, part, brick, sheet = (len(group) for group in (ELEC, PLANE, RING, PART, BRICK, SHEET))
     vmem = pl.BlockSpec(memory_space=pltpu.VMEM)
     return pl.pallas_call(
         kernel,
@@ -345,26 +341,26 @@
             pltpu.VMEM((count, columns), BF16),
             pltpu.VMEM((channels, LANES), BF16),
             pltpu.VMEM((channels, LANES + length), F32),
-            pltpu.VMEM((columns, length), BF16),
+            pltpu.VMEM((columns, length + LANES), BF16),
             pltpu.VMEM((part, 64, LANES + length), BF16),
             pltpu.VMEM((part, 64, LANES + length), BF16),
             pltpu.VMEM((8 * LANES, (part + 1) * length), BF16),
-            pltpu.VMEM((count, length), F32),
+            pltpu.VMEM((count, length + LANES), F32),
             pltpu.VMEM((near, 8, length), F32),
+            pltpu.VMEM((near + 1, 8, LANES), F32),
             pltpu.VMEM((part + 1, near + 1, 32, LANES), BF16),
             pltpu.VMEM((near + 1, 32, LANES), BF16),
             pltpu.VMEM((count, (part + 1) * length), BF16),
+            pltpu.VMEM((8, count, LANES), F32),
             pltpu.VMEM((ring, count, LANES), BF16),
             pltpu.VMEM((ring, count, LANES), BF16),
             pltpu.VMEM((LANES, LANES), F32),
-            pltpu.VMEM((part, 32, LANES), F32),
-            pltpu.VMEM((32, LANES), BF16),
-            pltpu.VMEM((ring, 32, LANES), BF16),
-            pltpu.VMEM((32, LANES), BF16),
-            pltpu.VMEM((near, 32, LANES), BF16),
+            pltpu.VMEM((brick, 8, LANES), F32),
+            pltpu.VMEM((8, LANES), F32),
+            pltpu.VMEM((sheet, 8, LANES), F32),
             pltpu.VMEM((LANES, LANES), F32),
             pltpu.SemaphoreType.DMA((2,)),
-            *sem_pairs(1, part, near, near, plane, 1, near, ring, part, ring, near, part),
+            *sem_pairs(1, part, near, near + 1, plane, 1, near, ring, brick, sheet, brick),
         ],
         compiler_params=pltpu.CompilerParams(
             collective_id=0, has_side_effects=True, vmem_limit_bytes=40 * 2**20

time: 67.7 us -> 68.4 us (1.010)
  Pallas kernels: 65.7 us -> 66.4 us
    pallas_call x1, Pallas kernels: 65.7 us -> 66.4 us  [shards(): pl.pallas_call(kernel, out_shape=(jax.ShapeDtypeStruct((count, length), B...]
where the time goes in v3:
time: 68.4 us; the launch traced here: 68.3 us
  Pallas kernels  66.4 us (97%)
  local copies, waits for them, and re-layouts  1.27 us (2%)
    pallas_call x1, Pallas kernels, shards(): pl.pallas_call(kernel, out_shape=(jax.ShapeDtypeStruct((count, length), B...  66.4 us

profile of v3, /device:TPU:1, one launch (start us, length us, event | category | flops | bytes accessed | tf_op | source)
XLA Modules:
  0.0 68.3 jit_solution(4885936519531811012)
XLA Ops:
  0.6 66.4 %separate.1 = (bf16[128,384]{1,0:T(8,128)(2,1)S(1)}, f32[128,128]{1,0:T(8,128)S(1)}) custom-call(bf16[256,384]{1,0:T(8,128)(2,1)} %sig_hbm.1, bf16[128,4096]{1,0:T(8,128)(2,1)} %vec_hbm.1), custom_call_target="tpu_custom_call" | custom-call | flops 1000000000 | bytes 2000000 | tf_op jit(solution)/shard_map/separate/pallas_call | solution.py:331
  67.0 0.6 copy.6
  67.7 0.6 copy.7

commit v4 on v3

--- a/solution.py
+++ b/solution.py
@@ -97,15 +97,24 @@
     return dot(jnp.concatenate([a1, a1, a2], 1), jnp.concatenate([a1, a2, a1], 1), both)
 
 
-def lagged(row):
-    return pltpu.roll(jnp.broadcast_to(row, (LAGS, LANES)), 0, 1, stride=1, stride_axis=0)
+def lagged(row, shift=0):
+    return pltpu.roll(jnp.broadcast_to(row, (LAGS, LANES)), shift, 1, stride=1, stride_axis=0)
+
+
+def packed(tile, shift):
+    return jnp.sum(pltpu.roll(tile, shift, 1, stride=LAGS, stride_axis=0), axis=0, keepdims=True)
+
+
+def before_first(row, r):
+    return lagged(row, (LANES - (r + 1) * LAGS) % LANES)
 
 
 def kernel(
     sig_hbm, vec_hbm, sources, unmixing,
-    sig, vec, tail, padded, ext, far_out, far_in, feat, partial, summed, spilled, blocks, waves, cubes,
+    sig, vec, wide, tail_out, tail_in, ext, far_out, far_in, late_out, late_in, feat,
+    partial, summed, spill_out, spill_in, blocks, waves, cubes,
     half, grad_out, grad_in, gram, gram_brick, gram_sum, gram_sheet, gram_all,
-    load, tail_s, tail_r, far_s, far_r, rs1_s, rs1_r, rs2_s, rs2_r, cube_s, cube_r, core_s, core_r, wave_s, wave_r,
+    load, tail_s, tail_r, far_s, far_r, late_s, late_r, rs1_s, rs1_r, rs2_s, rs2_r, cube_s, cube_r, core_s, core_r, wave_s, wave_r,
     grad_s, grad_r, g1_s, g1_r, g2_s, g2_r, g3_s, g3_r,
 ):
     at = place()
@@ -120,7 +129,7 @@
     ]
     for copy in loads:
         copy.start()
-    greeted = unique(PLANE + RING + PART + BRICK + SHEET)
+    greeted = unique(PLANE + RING + PART)
     barrier = pltpu.get_barrier_semaphore()
     for move in greeted:
         pl.semaphore_signal(barrier, inc=1, device_id=device(moved(at, move)), device_id_type=MESH)
@@ -145,6 +154,7 @@
 
     loads[1].wait()
     partial[...] = dot(vec[...], ext[...])
+    spill_out[...] = jnp.concatenate([packed(partial[8 * k : 8 * k + 8, length:], 0) for k in range(16)], 0)
     pl.semaphore_wait(barrier, len(greeted) + len(ELEC) + 1)
     rs_copies, spill_copies = [], []
     for i, move in enumerate(ELEC + [{}]):
@@ -154,45 +164,61 @@
             rs_copies.append(send(partial.at[rows, pl.ds(0, length)], summed.at[i], (rs1_s, rs1_r), i, device(to)))
         over = {"elec": elec_of(to), "tm": after}
         spill_copies.append(
-            send(partial.at[rows, pl.ds(length, LANES)], spilled.at[i], (rs2_s, rs2_r), i, over)
+            send(spill_out.at[pl.ds(elec_of(to), 1)], spill_in.at[pl.ds(i, 1)], (rs2_s, rs2_r), i, over)
         )
-    tail_copy = send(
-        sig.at[:, pl.ds(length - LANES, LANES)], tail, (tail_s, tail_r), 0, {"elec": elec, "tm": after}
+    wide[...] = sig[...].astype(F32)
+    last = lax.broadcasted_iota(jnp.int32, (8, LANES), 1) >= LANES - LAGS
+    tail_out[...] = jnp.concatenate(
+        [
+            packed(jnp.where(last, wide[8 * k : 8 * k + 8, length - LANES :], 0.0), LAGS)
+            for k in range(wide.shape[0] // 8)
+        ],
+        0,
     )
-
-    padded[:, LANES:] = sig[...].astype(F32)
+    tail_copy = send(tail_out, tail_in, (tail_s, tail_r), 0, {"elec": elec, "tm": after})
+
+    def start_of(to, z):
+        return to["l"] * 16 + z * 2 + to["c"]
+
+    for i, move in enumerate(PART):
+        to = moved(at, move)
+        starts = [pl.multiple_of(start_of(to, z) * 8, 8) for z in range(8)]
+        far_out[i] = jnp.concatenate([wide[pl.ds(start, 8), :] for start in starts], 0).astype(BF16)
     for z in range(8):
-        own = pl.multiple_of((at["l"] * 16 + z * 2 + at["c"]) * LANES, LANES)
+        own = pl.multiple_of(start_of(at, z) * LANES, LANES)
         feat[z * LANES : (z + 1) * LANES, :length] = ext[pl.ds(own, LANES), :length]
+    for copy in rs_copies:
+        copy.wait_send()
+    far_copies = [
+        send(far_out.at[i], far_in.at[i], (far_s, far_r), i, device(moved(at, move))) for i, move in enumerate(PART)
+    ]
     tail_copy.wait()
     first = jnp.where(tm > 0, 1.0, 0.0)
-    padded[:, :LANES] = tail[...].astype(F32) * first
-
-    far_copies = []
+    late_copies = []
     for i, move in enumerate(PART):
         to = moved(at, move)
-        starts = [pl.multiple_of((to["l"] * 16 + z * 2 + to["c"]) * 8, 8) for z in range(8)]
-        far_out[i] = jnp.concatenate([padded[pl.ds(start, 8), :] for start in starts], 0).astype(BF16)
-        far_copies.append(send(far_out.at[i], far_in.at[i], (far_s, far_r), i, device(to)))
+        late_out[i] = jnp.concatenate([tail_in[pl.ds(start_of(to, z), 1), :] for z in range(8)], 0) * first
+        late_copies.append(send(late_out.at[i], late_in.at[i], (late_s, late_r), i, device(to)))
 
     @pl.loop(0, 8)
     def _(z):
-        start = pl.multiple_of((at["l"] * 16 + z * 2 + at["c"]) * 8, 8)
-        rows = padded[pl.ds(start, 8), :LANES]
+        row = tail_in[pl.ds(start_of(at, z), 1), :] * first
         for r in range(8):
             to = pl.ds((z * 8 + r) * LAGS, LAGS)
-            feat[to, :LANES] = jnp.where(spill, lagged(rows[r : r + 1]), feat[to, :LANES].astype(F32)).astype(BF16)
+            feat[to, :LANES] = jnp.where(spill, before_first(row, r), feat[to, :LANES].astype(F32)).astype(BF16)
 
     mine = pl.ds(pl.multiple_of(elec * 8, 8), 8)
     total = partial[mine, :length]
-    for copy in rs_copies + spill_copies:
+    for copy in rs_copies:
+        copy.wait_recv()
+    for copy in spill_copies:
         copy.wait()
     for i in range(len(ELEC)):
         total = total + summed[i]
-    over = spilled[0]
-    for i in range(len(ELEC)):
-        over = over + spilled[i + 1]
-    total = jnp.concatenate([total[:, :LANES] + over * first, total[:, LANES:]], 1)
+    over = jnp.sum(spill_in[...], axis=0, keepdims=True) * first
+    over = jnp.concatenate([pltpu.roll(over, (LANES - r * LAGS) % LANES, 1) for r in range(8)], 0)
+    over = jnp.where(lax.broadcasted_iota(jnp.int32, (8, LANES), 1) < LAGS, over, 0.0)
+    total = jnp.concatenate([total[:, :LANES] + over, total[:, LANES:]], 1)
 
     def stacked(block, last):
         return jnp.concatenate([block[:, k * LANES : (k + 1) * LANES] for k in range(tiles)] + [last], 0).astype(BF16)
@@ -210,20 +236,18 @@
         cube_copies.append(
             send(blocks.at[0, elec], blocks.at[move["l"], elec], (cube_s, cube_r), i, device(moved(at, move)))
         )
-    wave_copies = [
-        send(waves.at[elec], waves.at[elec], (wave_s, wave_r), i, device(moved(at, move)))
-        for i, move in enumerate(ELEC)
-    ]
-
-    for i, copy in enumerate(far_copies):
-        copy.wait()
+    for i, (copy, late_copy) in enumerate(zip(far_copies, late_copies)):
+        copy.wait()
+        late_copy.wait()
 
         @pl.loop(0, 4)
         def _(block):
             rows = far_in[i, pl.ds(block * 16, 16), :].astype(F32)
+            ends = late_in[i, pl.ds(block * 2, 2), :]
             for r in range(16):
                 to = pl.ds((block * 16 + r) * LAGS, LAGS)
-                turned = [lagged(rows[r : r + 1, k * LANES : (k + 1) * LANES]) for k in range(tiles + 1)]
+                turned = [before_first(ends[r // 8 : r // 8 + 1], r % 8)]
+                turned += [lagged(rows[r : r + 1, k * LANES : (k + 1) * LANES]) for k in range(tiles)]
                 for k in range(tiles):
                     begin = (i + 1) * length + k * LANES
                     feat[to, begin : begin + LANES] = jnp.where(spill, turned[k], turned[k + 1]).astype(BF16)
@@ -262,6 +286,10 @@
         to = moved(at, move)
         grad_out[i] = block_of(to["z"]).astype(BF16)
         grad_copies.append(send(grad_out.at[i], grad_in.at[i], (grad_s, grad_r), i, device(to)))
+    wave_copies = [
+        send(waves.at[elec], waves.at[elec], (wave_s, wave_r), i, device(moved(at, move)))
+        for i, move in enumerate(ELEC)
+    ]
     updated = block_of(at["z"])
     for copy in wave_copies:
         copy.wait()
@@ -339,15 +367,19 @@
         scratch_shapes=[
             pltpu.VMEM((channels, length), BF16),
             pltpu.VMEM((count, columns), BF16),
-            pltpu.VMEM((channels, LANES), BF16),
-            pltpu.VMEM((channels, LANES + length), F32),
+            pltpu.VMEM((channels, length), F32),
+            pltpu.VMEM((channels // 8, LANES), F32),
+            pltpu.VMEM((channels // 8, LANES), F32),
             pltpu.VMEM((columns, length + LANES), BF16),
-            pltpu.VMEM((part, 64, LANES + length), BF16),
-            pltpu.VMEM((part, 64, LANES + length), BF16),
+            pltpu.VMEM((part, 64, length), BF16),
+            pltpu.VMEM((part, 64, length), BF16),
+            pltpu.VMEM((part, 8, LANES), F32),
+            pltpu.VMEM((part, 8, LANES), F32),
             pltpu.VMEM((8 * LANES, (part + 1) * length), BF16),
             pltpu.VMEM((count, length + LANES), F32),
             pltpu.VMEM((near, 8, length), F32),
-            pltpu.VMEM((near + 1, 8, LANES), F32),
+            pltpu.VMEM((near + 1, LANES), F32),
+            pltpu.VMEM((near + 1, LANES), F32),
             pltpu.VMEM((part + 1, near + 1, 32, LANES), BF16),
             pltpu.VMEM((near + 1, 32, LANES), BF16),
             pltpu.VMEM((count, (part + 1) * length), BF16),
@@ -360,7 +392,7 @@
             pltpu.VMEM((sheet, 8, LANES), F32),
             pltpu.VMEM((LANES, LANES), F32),
             pltpu.SemaphoreType.DMA((2,)),
-            *sem_pairs(1, part, near, near + 1, plane, 1, near, ring, brick, sheet, brick),
+            *sem_pairs(1, part, part, near, near + 1, plane, 1, near, ring, brick, sheet, brick),
         ],
         compiler_params=pltpu.CompilerParams(
             collective_id=0, has_side_effects=True, vmem_limit_bytes=40 * 2**20

time: 68.4 us -> 66.4 us (0.971)
  Pallas kernels: 66.4 us -> 64.3 us
    pallas_call x1, Pallas kernels: 66.4 us -> 64.3 us  [shards(): pl.pallas_call(kernel, out_shape=(jax.ShapeDtypeStruct((count, length), B...]
where the time goes in v4:
time: 66.4 us; the launch traced here: 66.2 us
  Pallas kernels  64.3 us (97%)
  local copies, waits for them, and re-layouts  1.27 us (2%)
    pallas_call x1, Pallas kernels, shards(): pl.pallas_call(kernel, out_shape=(jax.ShapeDtypeStruct((count, length), B...  64.3 us

profile of v4, /device:TPU:1, one launch (start us, length us, event | category | flops | bytes accessed | tf_op | source)
XLA Modules:
  0.0 66.2 jit_solution(1910503521209743538)
XLA Ops:
  0.6 64.3 %separate.1 = (bf16[128,384]{1,0:T(8,128)(2,1)S(1)}, f32[128,128]{1,0:T(8,128)S(1)}) custom-call(bf16[256,384]{1,0:T(8,128)(2,1)} %sig_hbm.1, bf16[128,4096]{1,0:T(8,128)(2,1)} %vec_hbm.1), custom_call_target="tpu_custom_call" | custom-call | flops 1000000000 | bytes 2000000 | tf_op jit(solution)/shard_map/separate/pallas_call | solution.py:359
  65.0 0.6 copy.6
  65.6 0.6 copy.7

commit v5 on v4

--- a/solution.py
+++ b/solution.py
@@ -64,17 +64,18 @@
     return {"elec": elec_of(at), "tm": tm_of(at)}
 
 
-def send(src, dst, sems, slot, to):
-    copy = pltpu.make_async_remote_copy(
+def remote(src, dst, sems, step, to):
+    return pltpu.make_async_remote_copy(
         src_ref=src,
         dst_ref=dst,
-        send_sem=sems[0].at[slot],
-        recv_sem=sems[1].at[slot],
+        send_sem=sems[0].at[step],
+        recv_sem=sems[1].at[step],
         device_id=to,
         device_id_type=MESH,
     )
-    copy.start()
-    return copy
+
+
+(TAIL, FAR, LATE, SUM, SPILL, CUBE, CORE, WAVE, GRAD, GRAM1, GRAM2, GRAM3) = range(12)
 
 
 def halves(a):
@@ -114,8 +115,7 @@
     sig, vec, wide, tail_out, tail_in, ext, far_out, far_in, late_out, late_in, feat,
     partial, summed, spill_out, spill_in, blocks, waves, cubes,
     half, grad_out, grad_in, gram, gram_brick, gram_sum, gram_sheet, gram_all,
-    load, tail_s, tail_r, far_s, far_r, late_s, late_r, rs1_s, rs1_r, rs2_s, rs2_r, cube_s, cube_r, core_s, core_r, wave_s, wave_r,
-    grad_s, grad_r, g1_s, g1_r, g2_s, g2_r, g3_s, g3_r,
+    load, sent, got,
 ):
     at = place()
     elec, tm = elec_of(at), tm_of(at)
@@ -129,6 +129,18 @@
     ]
     for copy in loads:
         copy.start()
+    sems = (sent, got)
+    partner = device(moved(at, PART[1]))
+
+    def send(src, dst, step, to):
+        remote(src, dst, sems, step, to).start()
+
+    def left(step, ref):
+        remote(ref, ref, sems, step, partner).wait_send()
+
+    def came(step, ref):
+        remote(ref, ref, sems, step, partner).wait_recv()
+
     greeted = unique(PLANE + RING + PART)
     barrier = pltpu.get_barrier_semaphore()
     for move in greeted:
@@ -156,16 +168,13 @@
     partial[...] = dot(vec[...], ext[...])
     spill_out[...] = jnp.concatenate([packed(partial[8 * k : 8 * k + 8, length:], 0) for k in range(16)], 0)
     pl.semaphore_wait(barrier, len(greeted) + len(ELEC) + 1)
-    rs_copies, spill_copies = [], []
     for i, move in enumerate(ELEC + [{}]):
         to = moved(at, move)
         rows = pl.ds(pl.multiple_of(elec_of(to) * 8, 8), 8)
         if move:
-            rs_copies.append(send(partial.at[rows, pl.ds(0, length)], summed.at[i], (rs1_s, rs1_r), i, device(to)))
+            send(partial.at[rows, pl.ds(0, length)], summed.at[i], SUM, device(to))
         over = {"elec": elec_of(to), "tm": after}
-        spill_copies.append(
-            send(spill_out.at[pl.ds(elec_of(to), 1)], spill_in.at[pl.ds(i, 1)], (rs2_s, rs2_r), i, over)
-        )
+        send(spill_out.at[pl.ds(elec_of(to), 1)], spill_in.at[pl.ds(i, 1)], SPILL, over)
     wide[...] = sig[...].astype(F32)
     last = lax.broadcasted_iota(jnp.int32, (8, LANES), 1) >= LANES - LAGS
     tail_out[...] = jnp.concatenate(
@@ -175,7 +184,7 @@
         ],
         0,
     )
-    tail_copy = send(tail_out, tail_in, (tail_s, tail_r), 0, {"elec": elec, "tm": after})
+    send(tail_out, tail_in, TAIL, {"elec": elec, "tm": after})
 
     def start_of(to, z):
         return to["l"] * 16 + z * 2 + to["c"]
@@ -187,18 +196,15 @@
     for z in range(8):
         own = pl.multiple_of(start_of(at, z) * LANES, LANES)
         feat[z * LANES : (z + 1) * LANES, :length] = ext[pl.ds(own, LANES), :length]
-    for copy in rs_copies:
-        copy.wait_send()
-    far_copies = [
-        send(far_out.at[i], far_in.at[i], (far_s, far_r), i, device(moved(at, move))) for i, move in enumerate(PART)
-    ]
-    tail_copy.wait()
+    left(SUM, summed)
+    for i, move in enumerate(PART):
+        send(far_out.at[i], far_in.at[i], FAR, device(moved(at, move)))
+    came(TAIL, tail_in)
     first = jnp.where(tm > 0, 1.0, 0.0)
-    late_copies = []
     for i, move in enumerate(PART):
         to = moved(at, move)
         late_out[i] = jnp.concatenate([tail_in[pl.ds(start_of(to, z), 1), :] for z in range(8)], 0) * first
-        late_copies.append(send(late_out.at[i], late_in.at[i], (late_s, late_r), i, device(to)))
+        send(late_out.at[i], late_in.at[i], LATE, device(to))
 
     @pl.loop(0, 8)
     def _(z):
@@ -209,10 +215,8 @@
 
     mine = pl.ds(pl.multiple_of(elec * 8, 8), 8)
     total = partial[mine, :length]
-    for copy in rs_copies:
-        copy.wait_recv()
-    for copy in spill_copies:
-        copy.wait()
+    came(SUM, summed)
+    came(SPILL, spill_in)
     for i in range(len(ELEC)):
         total = total + summed[i]
     over = jnp.sum(spill_in[...], axis=0, keepdims=True) * first
@@ -229,16 +233,13 @@
     low = deriv - high - middle
     lane = lax.broadcasted_iota(jnp.int32, (8, LANES), 1)
     pad = jnp.where(lane == 0, high, jnp.where(lane == 1, middle, jnp.where(lane == 2, low, 0.0)))
-    blocks[0, elec] = stacked(total * total * total, pad)
+    blocks[elec] = stacked(total * total * total, pad)
     waves[elec] = stacked(total, jnp.zeros((8, LANES), F32))
-    cube_copies = []
-    for i, move in enumerate(PLANE):
-        cube_copies.append(
-            send(blocks.at[0, elec], blocks.at[move["l"], elec], (cube_s, cube_r), i, device(moved(at, move)))
-        )
-    for i, (copy, late_copy) in enumerate(zip(far_copies, late_copies)):
-        copy.wait()
-        late_copy.wait()
+    for move in PLANE:
+        send(blocks.at[elec], blocks.at[elec + 16 * move["l"]], CUBE, device(moved(at, move)))
+    came(FAR, far_in)
+    came(LATE, late_in)
+    for i in range(len(PART)):
 
         @pl.loop(0, 4)
         def _(block):
@@ -252,14 +253,14 @@
                     begin = (i + 1) * length + k * LANES
                     feat[to, begin : begin + LANES] = jnp.where(spill, turned[k], turned[k + 1]).astype(BF16)
 
-    for copy in cube_copies:
-        copy.wait()
-    core_copy = send(blocks.at[pl.ds(0, 2)], blocks.at[pl.ds(2, 2)], (core_s, core_r), 0, device(moved(at, PART[1])))
+    came(CUBE, blocks.at[pl.ds(0, len(PLANE))])
+    left(CUBE, blocks.at[pl.ds(0, len(PLANE))])
+    send(blocks.at[pl.ds(0, 32)], blocks.at[pl.ds(32, 32)], CORE, partner)
 
     def unpack(shard):
         pads = []
         for pair in range(8):
-            pieces = [blocks[shard, 2 * pair + k].astype(F32) for k in range(2)]
+            pieces = [blocks[shard * 16 + 2 * pair + k].astype(F32) for k in range(2)]
             for k in range(tiles):
                 rows = jnp.concatenate([piece[8 * k : 8 * k + 8] for piece in pieces], 0)
                 begin = shard * length + k * LANES
@@ -271,7 +272,7 @@
     pads = unpack(0) + unpack(1)
     for z in range(8):
         half[z] = dot(cubes[:, : 2 * length], feat[z * LANES : (z + 1) * LANES, : 2 * length], both)
-    core_copy.wait()
+    came(CORE, blocks.at[pl.ds(32, 32)])
     pads = pads + unpack(2) + unpack(3)
     deriv = jnp.sum(pads, axis=1, keepdims=True)
 
@@ -281,55 +282,44 @@
         grad = half[z] + dot(cubes[:, 2 * length :], feat[rows, 2 * length :], both)
         return grad - deriv * vec[:, columns].astype(F32)
 
-    grad_copies = []
     for i, move in enumerate(RING):
         to = moved(at, move)
         grad_out[i] = block_of(to["z"]).astype(BF16)
-        grad_copies.append(send(grad_out.at[i], grad_in.at[i], (grad_s, grad_r), i, device(to)))
-    wave_copies = [
-        send(waves.at[elec], waves.at[elec], (wave_s, wave_r), i, device(moved(at, move)))
-        for i, move in enumerate(ELEC)
-    ]
+        send(grad_out.at[i], grad_in.at[i], GRAD, device(to))
+    for move in ELEC:
+        send(waves.at[elec], waves.at[elec], WAVE, device(moved(at, move)))
     updated = block_of(at["z"])
-    for copy in wave_copies:
-        copy.wait()
+    came(WAVE, waves.at[pl.ds(0, len(ELEC))])
     for pair in range(8):
         pieces = [waves[2 * pair + k].astype(F32) for k in range(2)]
         for k in range(tiles):
             rows = jnp.concatenate([piece[8 * k : 8 * k + 8] for piece in pieces], 0)
             sources[16 * pair : 16 * pair + 16, k * LANES : (k + 1) * LANES] = rows.astype(BF16)
-    for i, copy in enumerate(grad_copies):
-        copy.wait()
+    came(GRAD, grad_in)
+    for i in range(len(RING)):
         updated = updated + grad_in[i].astype(F32)
     updated = updated * (1.0 / (length * 32))
 
     gram[...] = fine_gram(updated)
     mine = pl.ds(pl.multiple_of(brick_of(at) * 8, 8), 8)
-    copies = []
     for i, move in enumerate(BRICK):
         to = moved(at, move)
         rows = pl.ds(pl.multiple_of(brick_of(to) * 8, 8), 8)
-        copies.append(send(gram.at[rows], gram_brick.at[i], (g1_s, g1_r), i, device(to)))
+        send(gram.at[rows], gram_brick.at[i], GRAM1, device(to))
     total = gram[mine, :]
-    for copy in copies:
-        copy.wait()
+    came(GRAM1, gram_brick)
     for i in range(len(BRICK)):
         total = total + gram_brick[i]
     gram_sum[...] = total
-    copies = [
-        send(gram_sum, gram_sheet.at[i], (g2_s, g2_r), i, device(moved(at, move))) for i, move in enumerate(SHEET)
-    ]
-    for copy in copies:
-        copy.wait()
+    for i, move in enumerate(SHEET):
+        send(gram_sum, gram_sheet.at[i], GRAM2, device(moved(at, move)))
+    came(GRAM2, gram_sheet)
     for i in range(len(SHEET)):
         total = total + gram_sheet[i]
     gram_all[mine, :] = total
-    copies = [
-        send(gram_all.at[mine], gram_all.at[mine], (g3_s, g3_r), i, device(moved(at, move)))
-        for i, move in enumerate(BRICK)
-    ]
-    for copy in copies:
-        copy.wait()
+    for move in BRICK:
+        send(gram_all.at[mine], gram_all.at[mine], GRAM3, device(moved(at, move)))
+    came(GRAM3, gram_all.at[pl.ds(0, 8 * len(BRICK))])
 
     g = gram_all[...]
     row = lax.broadcasted_iota(jnp.int32, (LANES, LANES), 0)
@@ -338,23 +328,30 @@
     squares = jnp.sum(jnp.sum(g * unit, axis=1, keepdims=True), axis=0, keepdims=True)
     scale = START * math.sqrt(LANES) * lax.rsqrt(squares + 1e-06)
     g = g * scale * scale
-    product = None
+    current = updated * scale
     for step in range(NS_STEPS):
         factor = 1.5 * unit - 0.5 * g
-        product = factor if product is None else fine_dot(factor, product)
+        current = fine_dot(factor, current)
         if step < NS_STEPS - 1:
             g = fine_dot(fine_dot(factor, g), factor)
-    unmixing[...] = fine_dot(product, updated * scale)
-
-
-def sem_pairs(*counts):
-    return [pltpu.SemaphoreType.DMA((count,)) for count in counts for _ in range(2)]
+    unmixing[...] = current
+
+    left(TAIL, tail_in)
+    left(FAR, far_in)
+    left(LATE, late_in)
+    left(SPILL, spill_in)
+    left(CORE, blocks.at[pl.ds(32, 32)])
+    left(WAVE, waves.at[pl.ds(0, len(ELEC))])
+    left(GRAD, grad_in)
+    left(GRAM1, gram_brick)
+    left(GRAM2, gram_sheet)
+    left(GRAM3, gram_all.at[pl.ds(0, 8 * len(BRICK))])
 
 
 def shards(signals, vectors):
     channels, length = signals.shape
     count, columns = vectors.shape
-    near, plane, ring, part, brick, sheet = (len(group) for group in (ELEC, PLANE, RING, PART, BRICK, SHEET))
+    near, ring, part, brick, sheet = (len(group) for group in (ELEC, RING, PART, BRICK, SHEET))
     vmem = pl.BlockSpec(memory_space=pltpu.VMEM)
     return pl.pallas_call(
         kernel,
@@ -380,7 +377,7 @@
             pltpu.VMEM((near, 8, length), F32),
             pltpu.VMEM((near + 1, LANES), F32),
             pltpu.VMEM((near + 1, LANES), F32),
-            pltpu.VMEM((part + 1, near + 1, 32, LANES), BF16),
+            pltpu.VMEM(((part + 1) * (near + 1), 32, LANES), BF16),
             pltpu.VMEM((near + 1, 32, LANES), BF16),
             pltpu.VMEM((count, (part + 1) * length), BF16),
             pltpu.VMEM((8, count, LANES), F32),
@@ -392,7 +389,8 @@
             pltpu.VMEM((sheet, 8, LANES), F32),
             pltpu.VMEM((LANES, LANES), F32),
             pltpu.SemaphoreType.DMA((2,)),
-            *sem_pairs(1, part, part, near, near + 1, plane, 1, near, ring, brick, sheet, brick),
+            pltpu.SemaphoreType.DMA((12,)),
+            pltpu.SemaphoreType.DMA((12,)),
         ],
         compiler_params=pltpu.CompilerParams(
             collective_id=0, has_side_effects=True, vmem_limit_bytes=40 * 2**20

time: 66.4 us -> 62.6 us (0.943)
  Pallas kernels: 64.3 us -> 60.6 us
    pallas_call x1, Pallas kernels: 64.3 us -> 60.6 us  [shards(): pl.pallas_call(kernel, out_shape=(jax.ShapeDtypeStruct((count, length), B...]
where the time goes in v5:
time: 62.6 us; the launch traced here: 62.5 us
  Pallas kernels  60.6 us (97%)
  local copies, waits for them, and re-layouts  1.27 us (2%)
  between operations  0.64 us (1%)
    pallas_call x1, Pallas kernels, shards(): pl.pallas_call(kernel, out_shape=(jax.ShapeDtypeStruct((count, length), B...  60.6 us
    unnamed x2, local copies, waits for them, and re-layouts  1.27 us

profile of v5, /device:TPU:1, one launch (start us, length us, event | category | flops | bytes accessed | tf_op | source)
XLA Modules:
  0.0 62.5 jit_solution(9292660674648714764)
XLA Ops:
  0.6 60.6 %separate.1 = (bf16[128,384]{1,0:T(8,128)(2,1)S(1)}, f32[128,128]{1,0:T(8,128)S(1)}) custom-call(bf16[256,384]{1,0:T(8,128)(2,1)} %sig_hbm.1, bf16[128,4096]{1,0:T(8,128)(2,1)} %vec_hbm.1), custom_call_target="tpu_custom_call" | custom-call | flops 1000000000 | bytes 2000000 | tf_op jit(solution)/shard_map/separate/pallas_call | solution.py:356
  61.2 0.6 %copy.6 = bf16[128,384]{1,0:T(8,128)(2,1)} copy(bf16[128,384]{1,0:T(8,128)(2,1)S(1)} %get-tuple-element.4) | data formatting | bytes 196608
  61.9 0.6 %copy.7 = f32[128,128]{1,0:T(8,128)} copy(f32[128,128]{1,0:T(8,128)S(1)} %get-tuple-element.5) | data formatting | bytes 131072

commit v6 on v5

--- a/solution.py
+++ b/solution.py
@@ -31,7 +31,7 @@
 
 ELEC, PLANE, RING = moves("x", "h"), moves("x", "h", "l"), moves("z")
 PART = [dict(l=1), dict(c=1), dict(l=1, c=1)]
-BRICK, SHEET = moves("x", "l", "c"), moves("z", "h")
+ROW, SHEET = moves("x", "l"), moves("z", "h")
 
 
 def unique(found):
@@ -56,8 +56,8 @@
     return (at["l"] * 8 + at["z"]) * 2 + at["c"]
 
 
-def brick_of(at):
-    return (at["x"] * 2 + at["l"]) * 2 + at["c"]
+def row_of(at):
+    return at["x"] * 2 + at["l"]
 
 
 def device(at):
@@ -75,7 +75,7 @@
     )
 
 
-(TAIL, FAR, LATE, SUM, SPILL, CUBE, CORE, WAVE, GRAD, GRAM1, GRAM2, GRAM3) = range(12)
+(TAIL, FAR, LATE, SUM, SPILL, CUBE, CROSS, CORE1, CORE2, WAVE, GRAD, GRAM1, GRAM2, GRAM3) = range(14)
 
 
 def halves(a):
@@ -114,7 +114,7 @@
     sig_hbm, vec_hbm, sources, unmixing,
     sig, vec, wide, tail_out, tail_in, ext, far_out, far_in, late_out, late_in, feat,
     partial, summed, spill_out, spill_in, blocks, waves, cubes,
-    half, grad_out, grad_in, gram, gram_brick, gram_sum, gram_sheet, gram_all,
+    half, grad_out, grad_in, gram, gram_row, gram_sum, gram_sheet, gram_all,
     load, sent, got,
 ):
     at = place()
@@ -143,11 +143,11 @@
 
     greeted = unique(PLANE + RING + PART)
     barrier = pltpu.get_barrier_semaphore()
-    for move in greeted:
-        pl.semaphore_signal(barrier, inc=1, device_id=device(moved(at, move)), device_id_type=MESH)
     for move in ELEC + [{}]:
         other = {"elec": elec_of(moved(at, move)), "tm": before}
         pl.semaphore_signal(barrier, inc=1, device_id=other, device_id_type=MESH)
+    for move in greeted:
+        pl.semaphore_signal(barrier, inc=1, device_id=device(moved(at, move)), device_id_type=MESH)
 
     lane = lax.broadcasted_iota(jnp.int32, (LAGS, LANES), 1)
     late = lax.broadcasted_iota(jnp.int32, (LAGS, LANES), 0)
@@ -235,8 +235,11 @@
     pad = jnp.where(lane == 0, high, jnp.where(lane == 1, middle, jnp.where(lane == 2, low, 0.0)))
     blocks[elec] = stacked(total * total * total, pad)
     waves[elec] = stacked(total, jnp.zeros((8, LANES), F32))
+    for move in ELEC:
+        send(blocks.at[elec], blocks.at[elec], CUBE, device(moved(at, move)))
     for move in PLANE:
-        send(blocks.at[elec], blocks.at[elec + 16 * move["l"]], CUBE, device(moved(at, move)))
+        if move["l"]:
+            send(blocks.at[elec], blocks.at[elec + 16], CROSS, device(moved(at, move)))
     came(FAR, far_in)
     came(LATE, late_in)
     for i in range(len(PART)):
@@ -253,10 +256,6 @@
                     begin = (i + 1) * length + k * LANES
                     feat[to, begin : begin + LANES] = jnp.where(spill, turned[k], turned[k + 1]).astype(BF16)
 
-    came(CUBE, blocks.at[pl.ds(0, len(PLANE))])
-    left(CUBE, blocks.at[pl.ds(0, len(PLANE))])
-    send(blocks.at[pl.ds(0, 32)], blocks.at[pl.ds(32, 32)], CORE, partner)
-
     def unpack(shard):
         pads = []
         for pair in range(8):
@@ -269,11 +268,18 @@
         return jnp.concatenate(pads, 0)
 
     both = (((1,), (1,)), ((), ()))
-    pads = unpack(0) + unpack(1)
+    came(CUBE, blocks.at[pl.ds(0, 15)])
+    send(blocks.at[pl.ds(0, 16)], blocks.at[pl.ds(32, 16)], CORE1, partner)
+    pads = unpack(0)
+    came(CROSS, blocks.at[pl.ds(16, 16)])
+    send(blocks.at[pl.ds(16, 16)], blocks.at[pl.ds(48, 16)], CORE2, partner)
+    pads = pads + unpack(1)
     for z in range(8):
         half[z] = dot(cubes[:, : 2 * length], feat[z * LANES : (z + 1) * LANES, : 2 * length], both)
-    came(CORE, blocks.at[pl.ds(32, 32)])
-    pads = pads + unpack(2) + unpack(3)
+    came(CORE1, blocks.at[pl.ds(32, 16)])
+    pads = pads + unpack(2)
+    came(CORE2, blocks.at[pl.ds(48, 16)])
+    pads = pads + unpack(3)
     deriv = jnp.sum(pads, axis=1, keepdims=True)
 
     def block_of(z):
@@ -301,25 +307,43 @@
     updated = updated * (1.0 / (length * 32))
 
     gram[...] = fine_gram(updated)
-    mine = pl.ds(pl.multiple_of(brick_of(at) * 8, 8), 8)
-    for i, move in enumerate(BRICK):
-        to = moved(at, move)
-        rows = pl.ds(pl.multiple_of(brick_of(to) * 8, 8), 8)
-        send(gram.at[rows], gram_brick.at[i], GRAM1, device(to))
-    total = gram[mine, :]
-    came(GRAM1, gram_brick)
-    for i in range(len(BRICK)):
-        total = total + gram_brick[i]
-    gram_sum[...] = total
-    for i, move in enumerate(SHEET):
-        send(gram_sum, gram_sheet.at[i], GRAM2, device(moved(at, move)))
-    came(GRAM2, gram_sheet)
-    for i in range(len(SHEET)):
-        total = total + gram_sheet[i]
-    gram_all[mine, :] = total
-    for move in BRICK:
-        send(gram_all.at[mine], gram_all.at[mine], GRAM3, device(moved(at, move)))
-    came(GRAM3, gram_all.at[pl.ds(0, 8 * len(BRICK))])
+    mine = pl.ds(pl.multiple_of(row_of(at) * 16, 16), 16)
+
+    def scatter(move, slot):
+        to = moved(at, move) | dict(c=1)
+        rows = pl.ds(pl.multiple_of(row_of(to) * 16, 16), 16)
+        send(gram.at[rows], gram_row.at[slot], GRAM1, device(to))
+
+    for i, move in enumerate(ROW):
+        scatter(move, i + 8 * at["c"])
+
+    @pl.when(at["c"] == 0)
+    def _():
+        scatter({}, len(ROW))
+
+    @pl.when(at["c"] == 1)
+    def _():
+        came(GRAM1, gram_row)
+        total = gram[mine, :]
+        for i in range(2 * len(ROW) + 1):
+            total = total + gram_row[i]
+        gram_sum[...] = total.astype(BF16)
+        for i, move in enumerate(SHEET):
+            send(gram_sum, gram_sheet.at[i], GRAM2, device(moved(at, move)))
+        came(GRAM2, gram_sheet)
+        total = gram_sum[...].astype(F32)
+        for i in range(len(SHEET)):
+            total = total + gram_sheet[i].astype(F32)
+        gram_all[mine, :] = total
+        for move in ROW + [{}]:
+            send(gram_all.at[mine], gram_all.at[mine], GRAM3, device(moved(at, move) | dict(c=0)))
+        for move in ROW:
+            send(gram_all.at[mine], gram_all.at[mine], GRAM3, device(moved(at, move)))
+        came(GRAM3, gram_all.at[pl.ds(0, 16 * len(ROW))])
+
+    @pl.when(at["c"] == 0)
+    def _():
+        came(GRAM3, gram_all)
 
     g = gram_all[...]
     row = lax.broadcasted_iota(jnp.int32, (LANES, LANES), 0)
@@ -340,18 +364,28 @@
     left(FAR, far_in)
     left(LATE, late_in)
     left(SPILL, spill_in)
-    left(CORE, blocks.at[pl.ds(32, 32)])
+    left(CUBE, blocks.at[pl.ds(0, 15)])
+    left(CROSS, blocks.at[pl.ds(0, 16)])
+    left(CORE1, blocks.at[pl.ds(0, 16)])
+    left(CORE2, blocks.at[pl.ds(0, 16)])
     left(WAVE, waves.at[pl.ds(0, len(ELEC))])
     left(GRAD, grad_in)
-    left(GRAM1, gram_brick)
-    left(GRAM2, gram_sheet)
-    left(GRAM3, gram_all.at[pl.ds(0, 8 * len(BRICK))])
+
+    @pl.when(at["c"] == 0)
+    def _():
+        left(GRAM1, gram_all)
+
+    @pl.when(at["c"] == 1)
+    def _():
+        left(GRAM1, gram_all.at[pl.ds(0, 16 * len(ROW))])
+        left(GRAM2, gram_sheet)
+        left(GRAM3, gram_row)
 
 
 def shards(signals, vectors):
     channels, length = signals.shape
     count, columns = vectors.shape
-    near, ring, part, brick, sheet = (len(group) for group in (ELEC, RING, PART, BRICK, SHEET))
+    near, ring, part, row, sheet = (len(group) for group in (ELEC, RING, PART, ROW, SHEET))
     vmem = pl.BlockSpec(memory_space=pltpu.VMEM)
     return pl.pallas_call(
         kernel,
@@ -384,13 +418,13 @@
             pltpu.VMEM((ring, count, LANES), BF16),
             pltpu.VMEM((ring, count, LANES), BF16),
             pltpu.VMEM((LANES, LANES), F32),
-            pltpu.VMEM((brick, 8, LANES), F32),
-            pltpu.VMEM((8, LANES), F32),
-            pltpu.VMEM((sheet, 8, LANES), F32),
+            pltpu.VMEM((2 * row + 1, 16, LANES), F32),
+            pltpu.VMEM((16, LANES), BF16),
+            pltpu.VMEM((sheet, 16, LANES), BF16),
             pltpu.VMEM((LANES, LANES), F32),
             pltpu.SemaphoreType.DMA((2,)),
-            pltpu.SemaphoreType.DMA((12,)),
-            pltpu.SemaphoreType.DMA((12,)),
+            pltpu.SemaphoreType.DMA((14,)),
+            pltpu.SemaphoreType.DMA((14,)),
         ],
         compiler_params=pltpu.CompilerParams(
             collective_id=0, has_side_effects=True, vmem_limit_bytes=40 * 2**20

time: 62.6 us -> 61 us (0.974)
  Pallas kernels: 60.6 us -> 59 us
    pallas_call x1, Pallas kernels: 60.6 us -> 59 us  [shards(): pl.pallas_call(kernel, out_shape=(jax.ShapeDtypeStruct((count, length), B...]
where the time goes in v6:
time: 61 us; the launch traced here: 60.9 us
  Pallas kernels  59 us (97%)
  local copies, waits for them, and re-layouts  1.27 us (2%)
  between operations  0.64 us (1%)
    pallas_call x1, Pallas kernels, shards(): pl.pallas_call(kernel, out_shape=(jax.ShapeDtypeStruct((count, length), B...  59 us
    unnamed x2, local copies, waits for them, and re-layouts  1.27 us

profile of v6, /device:TPU:1, one launch (start us, length us, event | category | flops | bytes accessed | tf_op | source)
XLA Modules:
  0.0 60.9 jit_solution(9758579014515887538)
XLA Ops:
  0.6 59.0 %separate.1 = (bf16[128,384]{1,0:T(8,128)(2,1)S(1)}, f32[128,128]{1,0:T(8,128)S(1)}) custom-call(bf16[256,384]{1,0:T(8,128)(2,1)} %sig_hbm.1, bf16[128,4096]{1,0:T(8,128)(2,1)} %vec_hbm.1), custom_call_target="tpu_custom_call" | custom-call | flops 1000000000 | bytes 2000000 | tf_op jit(solution)/shard_map/separate/pallas_call | solution.py:390
  59.6 0.6 %copy.6 = bf16[128,384]{1,0:T(8,128)(2,1)} copy(bf16[128,384]{1,0:T(8,128)(2,1)S(1)} %get-tuple-element.4) | data formatting | bytes 196608
  60.3 0.6 %copy.7 = f32[128,128]{1,0:T(8,128)} copy(f32[128,128]{1,0:T(8,128)S(1)} %get-tuple-element.5) | data formatting | bytes 131072

commit v7 on v6

--- a/solution.py
+++ b/solution.py
@@ -41,11 +41,11 @@
 
 def place():
     elec, tm = lax.axis_index("elec"), lax.axis_index("tm")
-    return dict(x=elec // 4, h=elec % 4, l=tm // 16, z=(tm // 2) % 8, c=tm % 2)
+    return dict(x=elec >> 2, h=elec & 3, l=tm >> 4, z=(tm >> 1) & 7, c=tm & 1)
 
 
 def moved(at, move):
-    return {k: lax.rem(v + move.get(k, 0), SIZE[k]) for k, v in at.items()}
+    return {k: (v + move[k]) & (SIZE[k] - 1) if move.get(k, 0) else v for k, v in at.items()}
 
 
 def elec_of(at):
@@ -75,7 +75,7 @@
     )
 
 
-(TAIL, FAR, LATE, SUM, SPILL, CUBE, CROSS, CORE1, CORE2, WAVE, GRAD, GRAM1, GRAM2, GRAM3) = range(14)
+(TAIL, FAR, LATE, SUM, SPILL, CUBE1, CUBE2, CORE1, CORE2, WAVE, GRAD1, GRAD2, GRAM1, GRAM2, GRAM3) = range(15)
 
 
 def halves(a):
@@ -121,7 +121,7 @@
     elec, tm = elec_of(at), tm_of(at)
     length = sig.shape[1]
     tiles = length // LANES
-    after, before = lax.rem(tm + 1, 32), lax.rem(tm + 31, 32)
+    after, before = (tm + 1) & 31, (tm + 31) & 31
 
     loads = [
         pltpu.make_async_copy(sig_hbm, sig, load.at[0]),
@@ -168,13 +168,20 @@
     partial[...] = dot(vec[...], ext[...])
     spill_out[...] = jnp.concatenate([packed(partial[8 * k : 8 * k + 8, length:], 0) for k in range(16)], 0)
     pl.semaphore_wait(barrier, len(greeted) + len(ELEC) + 1)
-    for i, move in enumerate(ELEC + [{}]):
-        to = moved(at, move)
+    for x, h in itertools.product(range(4), (2, 1, 3, 0)):
+        to = moved(at, dict(h=h)) | dict(x=x)
+        slot = at["x"] * 4 + h
         rows = pl.ds(pl.multiple_of(elec_of(to) * 8, 8), 8)
-        if move:
-            send(partial.at[rows, pl.ds(0, length)], summed.at[i], SUM, device(to))
+
+        def send_sum():
+            send(partial.at[rows, pl.ds(0, length)], summed.at[slot], SUM, device(to))
+
+        if h:
+            send_sum()
+        else:
+            pl.when(at["x"] != x)(send_sum)
         over = {"elec": elec_of(to), "tm": after}
-        send(spill_out.at[pl.ds(elec_of(to), 1)], spill_in.at[pl.ds(i, 1)], SPILL, over)
+        send(spill_out.at[pl.ds(elec_of(to), 1)], spill_in.at[pl.ds(slot, 1)], SPILL, over)
     wide[...] = sig[...].astype(F32)
     last = lax.broadcasted_iota(jnp.int32, (8, LANES), 1) >= LANES - LAGS
     tail_out[...] = jnp.concatenate(
@@ -196,7 +203,7 @@
     for z in range(8):
         own = pl.multiple_of(start_of(at, z) * LANES, LANES)
         feat[z * LANES : (z + 1) * LANES, :length] = ext[pl.ds(own, LANES), :length]
-    left(SUM, summed)
+    left(SUM, summed.at[pl.ds(0, 15)])
     for i, move in enumerate(PART):
         send(far_out.at[i], far_in.at[i], FAR, device(moved(at, move)))
     came(TAIL, tail_in)
@@ -214,11 +221,12 @@
             feat[to, :LANES] = jnp.where(spill, before_first(row, r), feat[to, :LANES].astype(F32)).astype(BF16)
 
     mine = pl.ds(pl.multiple_of(elec * 8, 8), 8)
-    total = partial[mine, :length]
-    came(SUM, summed)
+    summed[at["x"] * 4] = partial[mine, :length]
+    came(SUM, summed.at[pl.ds(0, 15)])
     came(SPILL, spill_in)
+    total = summed[0]
     for i in range(len(ELEC)):
-        total = total + summed[i]
+        total = total + summed[i + 1]
     over = jnp.sum(spill_in[...], axis=0, keepdims=True) * first
     over = jnp.concatenate([pltpu.roll(over, (LANES - r * LAGS) % LANES, 1) for r in range(8)], 0)
     over = jnp.where(lax.broadcasted_iota(jnp.int32, (8, LANES), 1) < LAGS, over, 0.0)
@@ -233,13 +241,13 @@
     low = deriv - high - middle
     lane = lax.broadcasted_iota(jnp.int32, (8, LANES), 1)
     pad = jnp.where(lane == 0, high, jnp.where(lane == 1, middle, jnp.where(lane == 2, low, 0.0)))
-    blocks[elec] = stacked(total * total * total, pad)
+    upper = at["x"] < 2
+    own = (at["x"] >> 1) * 32 + (elec & 7)
+    cube = CUBE1 + (at["x"] >> 1)
+    blocks[own] = stacked(total * total * total, pad)
     waves[elec] = stacked(total, jnp.zeros((8, LANES), F32))
-    for move in ELEC:
-        send(blocks.at[elec], blocks.at[elec], CUBE, device(moved(at, move)))
     for move in PLANE:
-        if move["l"]:
-            send(blocks.at[elec], blocks.at[elec + 16], CROSS, device(moved(at, move)))
+        send(blocks.at[own], blocks.at[own + 8 * move["l"]], cube, device(moved(at, move)))
     came(FAR, far_in)
     came(LATE, late_in)
     for i in range(len(PART)):
@@ -256,55 +264,64 @@
                     begin = (i + 1) * length + k * LANES
                     feat[to, begin : begin + LANES] = jnp.where(spill, turned[k], turned[k + 1]).astype(BF16)
 
-    def unpack(shard):
+    both = (((1,), (1,)), ((), ()))
+
+    def unpack(part, shard):
         pads = []
-        for pair in range(8):
-            pieces = [blocks[shard * 16 + 2 * pair + k].astype(F32) for k in range(2)]
+        for pair in range(4):
+            pieces = [blocks[part * 32 + shard * 8 + 2 * pair + k].astype(F32) for k in range(2)]
             for k in range(tiles):
                 rows = jnp.concatenate([piece[8 * k : 8 * k + 8] for piece in pieces], 0)
                 begin = shard * length + k * LANES
-                cubes[16 * pair : 16 * pair + 16, begin : begin + LANES] = rows.astype(BF16)
+                cubes[64 * part + 16 * pair : 64 * part + 16 * pair + 16, begin : begin + LANES] = rows.astype(BF16)
             pads += [piece[8 * tiles :] for piece in pieces]
         return jnp.concatenate(pads, 0)
 
-    both = (((1,), (1,)), ((), ()))
-    came(CUBE, blocks.at[pl.ds(0, 15)])
-    send(blocks.at[pl.ds(0, 16)], blocks.at[pl.ds(32, 16)], CORE1, partner)
-    pads = unpack(0)
-    came(CROSS, blocks.at[pl.ds(16, 16)])
-    send(blocks.at[pl.ds(16, 16)], blocks.at[pl.ds(48, 16)], CORE2, partner)
-    pads = pads + unpack(1)
-    for z in range(8):
-        half[z] = dot(cubes[:, : 2 * length], feat[z * LANES : (z + 1) * LANES, : 2 * length], both)
-    came(CORE1, blocks.at[pl.ds(32, 16)])
-    pads = pads + unpack(2)
-    came(CORE2, blocks.at[pl.ds(48, 16)])
-    pads = pads + unpack(3)
-    deriv = jnp.sum(pads, axis=1, keepdims=True)
-
-    def block_of(z):
-        rows = pl.ds(pl.multiple_of(z * LANES, LANES), LANES)
-        columns = pl.ds(pl.multiple_of((at["l"] * 16 + z * 2 + at["c"]) * LANES, LANES), LANES)
-        grad = half[z] + dot(cubes[:, 2 * length :], feat[rows, 2 * length :], both)
-        return grad - deriv * vec[:, columns].astype(F32)
-
-    for i, move in enumerate(RING):
-        to = moved(at, move)
-        grad_out[i] = block_of(to["z"]).astype(BF16)
-        send(grad_out.at[i], grad_in.at[i], GRAD, device(to))
+    own_grads = []
+    for part in range(2):
+        near, far = pl.ds(part * 32, 16), pl.ds(part * 32 + 16, 16)
+        mixed = upper if part == 0 else jnp.logical_not(upper)
+
+        @pl.when(mixed)
+        def _():
+            came(CUBE1 + part, blocks.at[pl.ds(0, 15)])
+
+        @pl.when(jnp.logical_not(mixed))
+        def _():
+            came(CUBE1 + part, blocks.at[pl.ds(0, 16)])
+
+        send(blocks.at[near], blocks.at[far], CORE1 + part, partner)
+        these = slice(64 * part, 64 * part + 64)
+        pads = unpack(part, 0) + unpack(part, 1)
+        half[...] = dot(cubes[these, : 2 * length], feat[:, : 2 * length], both)
+        came(CORE1 + part, blocks.at[far])
+        pads = pads + unpack(part, 2) + unpack(part, 3)
+        deriv = jnp.sum(pads, axis=1, keepdims=True)
+
+        def block_of(z):
+            rows = pl.ds(pl.multiple_of(z * LANES, LANES), LANES)
+            columns = pl.ds(pl.multiple_of(start_of(at, z) * LANES, LANES), LANES)
+            grad = half[:, rows] + dot(cubes[these, 2 * length :], feat[rows, 2 * length :], both)
+            return grad - deriv * vec[these, columns].astype(F32)
+
+        for i, move in enumerate(RING):
+            to = moved(at, move)
+            grad_out[part, i] = block_of(to["z"]).astype(BF16)
+            send(grad_out.at[part, i], grad_in.at[part, i], GRAD1 + part, device(to))
+        own_grads.append(block_of(at["z"]))
     for move in ELEC:
         send(waves.at[elec], waves.at[elec], WAVE, device(moved(at, move)))
-    updated = block_of(at["z"])
     came(WAVE, waves.at[pl.ds(0, len(ELEC))])
     for pair in range(8):
         pieces = [waves[2 * pair + k].astype(F32) for k in range(2)]
         for k in range(tiles):
             rows = jnp.concatenate([piece[8 * k : 8 * k + 8] for piece in pieces], 0)
             sources[16 * pair : 16 * pair + 16, k * LANES : (k + 1) * LANES] = rows.astype(BF16)
-    came(GRAD, grad_in)
-    for i in range(len(RING)):
-        updated = updated + grad_in[i].astype(F32)
-    updated = updated * (1.0 / (length * 32))
+    for part in range(2):
+        came(GRAD1 + part, grad_in.at[part])
+        for i in range(len(RING)):
+            own_grads[part] = own_grads[part] + grad_in[part, i].astype(F32)
+    updated = jnp.concatenate(own_grads, 0) * (1.0 / (length * 32))
 
     gram[...] = fine_gram(updated)
     mine = pl.ds(pl.multiple_of(row_of(at) * 16, 16), 16)
@@ -364,12 +381,12 @@
     left(FAR, far_in)
     left(LATE, late_in)
     left(SPILL, spill_in)
-    left(CUBE, blocks.at[pl.ds(0, 15)])
-    left(CROSS, blocks.at[pl.ds(0, 16)])
+    left(cube, blocks.at[pl.ds(0, len(PLANE))])
     left(CORE1, blocks.at[pl.ds(0, 16)])
     left(CORE2, blocks.at[pl.ds(0, 16)])
     left(WAVE, waves.at[pl.ds(0, len(ELEC))])
-    left(GRAD, grad_in)
+    left(GRAD1, grad_in.at[0])
+    left(GRAD2, grad_in.at[1])
 
     @pl.when(at["c"] == 0)
     def _():
@@ -408,23 +425,23 @@
             pltpu.VMEM((part, 8, LANES), F32),
             pltpu.VMEM((8 * LANES, (part + 1) * length), BF16),
             pltpu.VMEM((count, length + LANES), F32),
-            pltpu.VMEM((near, 8, length), F32),
+            pltpu.VMEM((near + 1, 8, length), F32),
             pltpu.VMEM((near + 1, LANES), F32),
             pltpu.VMEM((near + 1, LANES), F32),
             pltpu.VMEM(((part + 1) * (near + 1), 32, LANES), BF16),
             pltpu.VMEM((near + 1, 32, LANES), BF16),
             pltpu.VMEM((count, (part + 1) * length), BF16),
-            pltpu.VMEM((8, count, LANES), F32),
-            pltpu.VMEM((ring, count, LANES), BF16),
-            pltpu.VMEM((ring, count, LANES), BF16),
+            pltpu.VMEM((count // 2, 8 * LANES), F32),
+            pltpu.VMEM((2, ring, count // 2, LANES), BF16),
+            pltpu.VMEM((2, ring, count // 2, LANES), BF16),
             pltpu.VMEM((LANES, LANES), F32),
             pltpu.VMEM((2 * row + 1, 16, LANES), F32),
             pltpu.VMEM((16, LANES), BF16),
             pltpu.VMEM((sheet, 16, LANES), BF16),
             pltpu.VMEM((LANES, LANES), F32),
             pltpu.SemaphoreType.DMA((2,)),
-            pltpu.SemaphoreType.DMA((14,)),
-            pltpu.SemaphoreType.DMA((14,)),
+            pltpu.SemaphoreType.DMA((15,)),
+            pltpu.SemaphoreType.DMA((15,)),
         ],
         compiler_params=pltpu.CompilerParams(
             collective_id=0, has_side_effects=True, vmem_limit_bytes=40 * 2**20

time: 61 us -> 62.2 us (1.020)
  Pallas kernels: 59 us -> 60.1 us
    pallas_call x1, Pallas kernels: 59 us -> 60.1 us  [shards(): pl.pallas_call(kernel, out_shape=(jax.ShapeDtypeStruct((count, length), B...]
where the time goes in v7:
time: 62.2 us; the launch traced here: 62 us
  Pallas kernels  60.1 us (97%)
  local copies, waits for them, and re-layouts  1.27 us (2%)
  between operations  0.64 us (1%)
    pallas_call x1, Pallas kernels, shards(): pl.pallas_call(kernel, out_shape=(jax.ShapeDtypeStruct((count, length), B...  60.1 us
    unnamed x2, local copies, waits for them, and re-layouts  1.27 us

profile of v7, /device:TPU:1, one launch (start us, length us, event | category | flops | bytes accessed | tf_op | source)
XLA Modules:
  0.0 62.0 jit_solution(3636527693922210819)
XLA Ops:
  0.6 60.1 %separate.1 = (bf16[128,384]{1,0:T(8,128)(2,1)S(1)}, f32[128,128]{1,0:T(8,128)S(1)}) custom-call(bf16[256,384]{1,0:T(8,128)(2,1)} %sig_hbm.1, bf16[128,4096]{1,0:T(8,128)(2,1)} %vec_hbm.1), custom_call_target="tpu_custom_call" | custom-call | flops 1000000000 | bytes 2000000 | tf_op jit(solution)/shard_map/separate/pallas_call | solution.py:407
  60.7 0.6 %copy.6 = bf16[128,384]{1,0:T(8,128)(2,1)} copy(bf16[128,384]{1,0:T(8,128)(2,1)S(1)} %get-tuple-element.4) | data formatting | bytes 196608
  61.4 0.6 %copy.7 = f32[128,128]{1,0:T(8,128)} copy(f32[128,128]{1,0:T(8,128)S(1)} %get-tuple-element.5) | data formatting | bytes 131072

commit v8 on v6

--- a/solution.py
+++ b/solution.py
@@ -30,22 +30,17 @@
 
 
 ELEC, PLANE, RING = moves("x", "h"), moves("x", "h", "l"), moves("z")
-PART = [dict(l=1), dict(c=1), dict(l=1, c=1)]
+PART = [dict(c=1), dict(l=1), dict(l=1, c=1)]
 ROW, SHEET = moves("x", "l"), moves("z", "h")
-
-
-def unique(found):
-    seen = {tuple(move.get(name, 0) for name in SIZE): None for move in found}
-    return [dict(zip(SIZE, move)) for move in seen]
 
 
 def place():
     elec, tm = lax.axis_index("elec"), lax.axis_index("tm")
-    return dict(x=elec // 4, h=elec % 4, l=tm // 16, z=(tm // 2) % 8, c=tm % 2)
+    return dict(x=elec >> 2, h=elec & 3, l=tm >> 4, z=(tm >> 1) & 7, c=tm & 1)
 
 
 def moved(at, move):
-    return {k: lax.rem(v + move.get(k, 0), SIZE[k]) for k, v in at.items()}
+    return {k: (v + move[k]) & (SIZE[k] - 1) if move.get(k, 0) else v for k, v in at.items()}
 
 
 def elec_of(at):
@@ -113,7 +108,7 @@
 def kernel(
     sig_hbm, vec_hbm, sources, unmixing,
     sig, vec, wide, tail_out, tail_in, ext, far_out, far_in, late_out, late_in, feat,
-    partial, summed, spill_out, spill_in, blocks, waves, cubes,
+    partial, summed, spill_out, spill_in, blocks, wave_out, waves, cubes,
     half, grad_out, grad_in, gram, gram_row, gram_sum, gram_sheet, gram_all,
     load, sent, got,
 ):
@@ -121,7 +116,8 @@
     elec, tm = elec_of(at), tm_of(at)
     length = sig.shape[1]
     tiles = length // LANES
-    after, before = lax.rem(tm + 1, 32), lax.rem(tm + 31, 32)
+    after, before = (tm + 1) & 31, (tm + 31) & 31
+    core = at["c"]
 
     loads = [
         pltpu.make_async_copy(sig_hbm, sig, load.at[0]),
@@ -130,7 +126,7 @@
     for copy in loads:
         copy.start()
     sems = (sent, got)
-    partner = device(moved(at, PART[1]))
+    partner = device(moved(at, dict(c=1)))
 
     def send(src, dst, step, to):
         remote(src, dst, sems, step, to).start()
@@ -141,13 +137,26 @@
     def came(step, ref):
         remote(ref, ref, sems, step, partner).wait_recv()
 
-    greeted = unique(PLANE + RING + PART)
     barrier = pltpu.get_barrier_semaphore()
-    for move in ELEC + [{}]:
-        other = {"elec": elec_of(moved(at, move)), "tm": before}
-        pl.semaphore_signal(barrier, inc=1, device_id=other, device_id_type=MESH)
-    for move in greeted:
-        pl.semaphore_signal(barrier, inc=1, device_id=device(moved(at, move)), device_id_type=MESH)
+
+    def greet(to):
+        pl.semaphore_signal(barrier, inc=1, device_id=to, device_id_type=MESH)
+
+    @pl.when(core == 1)
+    def _():
+        for move in ELEC + [{}]:
+            to = moved(at, move)
+            greet({"elec": elec_of(to), "tm": (tm + 30) & 31})
+            greet(device(to | dict(c=0)))
+        for move in PLANE:
+            greet(device(moved(at, move)))
+
+    @pl.when(core == 0)
+    def _():
+        greet({"elec": elec, "tm": before})
+
+    for move in RING + PART:
+        greet(device(moved(at, move)))
 
     lane = lax.broadcasted_iota(jnp.int32, (LAGS, LANES), 1)
     late = lax.broadcasted_iota(jnp.int32, (LAGS, LANES), 0)
@@ -167,14 +176,30 @@
     loads[1].wait()
     partial[...] = dot(vec[...], ext[...])
     spill_out[...] = jnp.concatenate([packed(partial[8 * k : 8 * k + 8, length:], 0) for k in range(16)], 0)
-    pl.semaphore_wait(barrier, len(greeted) + len(ELEC) + 1)
+    every = len(RING) + len(PART) + len(ELEC) + 1
+
+    @pl.when(core == 1)
+    def _():
+        pl.semaphore_wait(barrier, every + len(PLANE) + 1)
+
+    @pl.when(core == 0)
+    def _():
+        pl.semaphore_wait(barrier, every)
+
+    onward = (tm + 1 + core) & 31
     for i, move in enumerate(ELEC + [{}]):
-        to = moved(at, move)
+        to = moved(at, move) | dict(c=1)
         rows = pl.ds(pl.multiple_of(elec_of(to) * 8, 8), 8)
+
+        def send_sum():
+            send(partial.at[rows, pl.ds(0, length)], summed.at[i + 16 * core], SUM, device(to))
+
         if move:
-            send(partial.at[rows, pl.ds(0, length)], summed.at[i], SUM, device(to))
-        over = {"elec": elec_of(to), "tm": after}
-        send(spill_out.at[pl.ds(elec_of(to), 1)], spill_in.at[pl.ds(i, 1)], SPILL, over)
+            send_sum()
+        else:
+            pl.when(core == 0)(send_sum)
+        over = {"elec": elec_of(to), "tm": onward}
+        send(spill_out.at[pl.ds(elec_of(to), 1)], spill_in.at[pl.ds(i + 16 * (1 - core), 1)], SPILL, over)
     wide[...] = sig[...].astype(F32)
     last = lax.broadcasted_iota(jnp.int32, (8, LANES), 1) >= LANES - LAGS
     tail_out[...] = jnp.concatenate(
@@ -196,7 +221,15 @@
     for z in range(8):
         own = pl.multiple_of(start_of(at, z) * LANES, LANES)
         feat[z * LANES : (z + 1) * LANES, :length] = ext[pl.ds(own, LANES), :length]
-    left(SUM, summed)
+
+    @pl.when(core == 0)
+    def _():
+        left(SUM, summed.at[pl.ds(0, 16)])
+
+    @pl.when(core == 1)
+    def _():
+        left(SUM, summed.at[pl.ds(0, 15)])
+
     for i, move in enumerate(PART):
         send(far_out.at[i], far_in.at[i], FAR, device(moved(at, move)))
     came(TAIL, tail_in)
@@ -213,33 +246,40 @@
             to = pl.ds((z * 8 + r) * LAGS, LAGS)
             feat[to, :LANES] = jnp.where(spill, before_first(row, r), feat[to, :LANES].astype(F32)).astype(BF16)
 
-    mine = pl.ds(pl.multiple_of(elec * 8, 8), 8)
-    total = partial[mine, :length]
-    came(SUM, summed)
-    came(SPILL, spill_in)
-    for i in range(len(ELEC)):
-        total = total + summed[i]
-    over = jnp.sum(spill_in[...], axis=0, keepdims=True) * first
-    over = jnp.concatenate([pltpu.roll(over, (LANES - r * LAGS) % LANES, 1) for r in range(8)], 0)
-    over = jnp.where(lax.broadcasted_iota(jnp.int32, (8, LANES), 1) < LAGS, over, 0.0)
-    total = jnp.concatenate([total[:, :LANES] + over, total[:, LANES:]], 1)
-
     def stacked(block, last):
         return jnp.concatenate([block[:, k * LANES : (k + 1) * LANES] for k in range(tiles)] + [last], 0).astype(BF16)
 
-    deriv = jnp.sum(3.0 * total * total, axis=1, keepdims=True)
-    high = deriv.astype(BF16).astype(F32)
-    middle = (deriv - high).astype(BF16).astype(F32)
-    low = deriv - high - middle
-    lane = lax.broadcasted_iota(jnp.int32, (8, LANES), 1)
-    pad = jnp.where(lane == 0, high, jnp.where(lane == 1, middle, jnp.where(lane == 2, low, 0.0)))
-    blocks[elec] = stacked(total * total * total, pad)
-    waves[elec] = stacked(total, jnp.zeros((8, LANES), F32))
-    for move in ELEC:
-        send(blocks.at[elec], blocks.at[elec], CUBE, device(moved(at, move)))
-    for move in PLANE:
-        if move["l"]:
-            send(blocks.at[elec], blocks.at[elec + 16], CROSS, device(moved(at, move)))
+    @pl.when(core == 1)
+    def _():
+        mine = pl.ds(pl.multiple_of(elec * 8, 8), 8)
+        lane = lax.broadcasted_iota(jnp.int32, (8, LANES), 1)
+        came(SUM, summed)
+        came(SPILL, spill_in)
+        for shard in range(2):
+            total = summed[15] if shard == 0 else partial[mine, :length]
+            for i in range(len(ELEC)):
+                total = total + summed[i + 16 * shard]
+            over = jnp.sum(spill_in[16 * shard : 16 * shard + 16], axis=0, keepdims=True)
+            if shard == 0:
+                over = over * jnp.where(tm > 1, 1.0, 0.0)
+            over = jnp.concatenate([pltpu.roll(over, (LANES - r * LAGS) % LANES, 1) for r in range(8)], 0)
+            over = jnp.where(lane < LAGS, over, 0.0)
+            total = jnp.concatenate([total[:, :LANES] + over, total[:, LANES:]], 1)
+            deriv = jnp.sum(3.0 * total * total, axis=1, keepdims=True)
+            high = deriv.astype(BF16).astype(F32)
+            middle = (deriv - high).astype(BF16).astype(F32)
+            low = deriv - high - middle
+            pad = jnp.where(lane == 0, high, jnp.where(lane == 1, middle, jnp.where(lane == 2, low, 0.0)))
+            blocks[2 * elec + shard] = stacked(total * total * total, pad)
+            wave_out[shard] = stacked(total, jnp.zeros((8, LANES), F32))
+        own = pl.ds(2 * elec, 2)
+        for move in ELEC:
+            send(blocks.at[own], blocks.at[own], CUBE, device(moved(at, move)))
+        for move in PLANE:
+            if move["l"]:
+                send(blocks.at[own], blocks.at[pl.ds(2 * elec + 32, 2)], CROSS, device(moved(at, move)))
+        waves[elec] = wave_out[1]
+
     came(FAR, far_in)
     came(LATE, late_in)
     for i in range(len(PART)):
@@ -257,9 +297,10 @@
                     feat[to, begin : begin + LANES] = jnp.where(spill, turned[k], turned[k + 1]).astype(BF16)
 
     def unpack(shard):
+        begin_at = 32 * (shard // 2) + (1 - core if shard % 2 else core)
         pads = []
         for pair in range(8):
-            pieces = [blocks[shard * 16 + 2 * pair + k].astype(F32) for k in range(2)]
+            pieces = [blocks[begin_at + 2 * (2 * pair + k)].astype(F32) for k in range(2)]
             for k in range(tiles):
                 rows = jnp.concatenate([piece[8 * k : 8 * k + 8] for piece in pieces], 0)
                 begin = shard * length + k * LANES
@@ -268,18 +309,31 @@
         return jnp.concatenate(pads, 0)
 
     both = (((1,), (1,)), ((), ()))
-    came(CUBE, blocks.at[pl.ds(0, 15)])
-    send(blocks.at[pl.ds(0, 16)], blocks.at[pl.ds(32, 16)], CORE1, partner)
-    pads = unpack(0)
-    came(CROSS, blocks.at[pl.ds(16, 16)])
-    send(blocks.at[pl.ds(16, 16)], blocks.at[pl.ds(48, 16)], CORE2, partner)
-    pads = pads + unpack(1)
+    near, far = pl.ds(0, 32), pl.ds(32, 32)
+
+    @pl.when(core == 1)
+    def _():
+        came(CUBE, blocks.at[pl.ds(0, 30)])
+        send(blocks.at[near], blocks.at[near], CORE1, partner)
+
+    @pl.when(core == 0)
+    def _():
+        came(CORE1, blocks.at[near])
+
+    pads = unpack(0) + unpack(1)
     for z in range(8):
         half[z] = dot(cubes[:, : 2 * length], feat[z * LANES : (z + 1) * LANES, : 2 * length], both)
-    came(CORE1, blocks.at[pl.ds(32, 16)])
-    pads = pads + unpack(2)
-    came(CORE2, blocks.at[pl.ds(48, 16)])
-    pads = pads + unpack(3)
+
+    @pl.when(core == 1)
+    def _():
+        came(CROSS, blocks.at[far])
+        send(blocks.at[far], blocks.at[far], CORE2, partner)
+
+    @pl.when(core == 0)
+    def _():
+        came(CORE2, blocks.at[far])
+
+    pads = pads + unpack(2) + unpack(3)
     deriv = jnp.sum(pads, axis=1, keepdims=True)
 
     def block_of(z):
@@ -292,10 +346,24 @@
         to = moved(at, move)
         grad_out[i] = block_of(to["z"]).astype(BF16)
         send(grad_out.at[i], grad_in.at[i], GRAD, device(to))
-    for move in ELEC:
-        send(waves.at[elec], waves.at[elec], WAVE, device(moved(at, move)))
+
+    @pl.when(core == 1)
+    def _():
+        for move in ELEC + [{}]:
+            send(wave_out.at[0], waves.at[elec], WAVE, device(moved(at, move) | dict(c=0)))
+        for move in ELEC:
+            send(wave_out.at[1], waves.at[elec], WAVE, device(moved(at, move)))
+
     updated = block_of(at["z"])
-    came(WAVE, waves.at[pl.ds(0, len(ELEC))])
+
+    @pl.when(core == 0)
+    def _():
+        came(WAVE, waves)
+
+    @pl.when(core == 1)
+    def _():
+        came(WAVE, waves.at[pl.ds(0, len(ELEC))])
+
     for pair in range(8):
         pieces = [waves[2 * pair + k].astype(F32) for k in range(2)]
         for k in range(tiles):
@@ -315,13 +383,13 @@
         send(gram.at[rows], gram_row.at[slot], GRAM1, device(to))
 
     for i, move in enumerate(ROW):
-        scatter(move, i + 8 * at["c"])
-
-    @pl.when(at["c"] == 0)
+        scatter(move, i + 8 * core)
+
+    @pl.when(core == 0)
     def _():
         scatter({}, len(ROW))
 
-    @pl.when(at["c"] == 1)
+    @pl.when(core == 1)
     def _():
         came(GRAM1, gram_row)
         total = gram[mine, :]
@@ -341,7 +409,7 @@
             send(gram_all.at[mine], gram_all.at[mine], GRAM3, device(moved(at, move)))
         came(GRAM3, gram_all.at[pl.ds(0, 16 * len(ROW))])
 
-    @pl.when(at["c"] == 0)
+    @pl.when(core == 0)
     def _():
         came(GRAM3, gram_all)
 
@@ -363,23 +431,23 @@
     left(TAIL, tail_in)
     left(FAR, far_in)
     left(LATE, late_in)
-    left(SPILL, spill_in)
-    left(CUBE, blocks.at[pl.ds(0, 15)])
-    left(CROSS, blocks.at[pl.ds(0, 16)])
-    left(CORE1, blocks.at[pl.ds(0, 16)])
-    left(CORE2, blocks.at[pl.ds(0, 16)])
-    left(WAVE, waves.at[pl.ds(0, len(ELEC))])
+    left(SPILL, spill_out)
     left(GRAD, grad_in)
 
-    @pl.when(at["c"] == 0)
+    @pl.when(core == 0)
     def _():
         left(GRAM1, gram_all)
 
-    @pl.when(at["c"] == 1)
+    @pl.when(core == 1)
     def _():
         left(GRAM1, gram_all.at[pl.ds(0, 16 * len(ROW))])
         left(GRAM2, gram_sheet)
         left(GRAM3, gram_row)
+        left(CUBE, blocks.at[pl.ds(0, 30)])
+        left(CROSS, blocks.at[pl.ds(0, 32)])
+        left(CORE1, blocks.at[pl.ds(0, 32)])
+        left(CORE2, blocks.at[pl.ds(0, 32)])
+        left(WAVE, blocks.at[pl.ds(0, 31)])
 
 
 def shards(signals, vectors):
@@ -408,10 +476,11 @@
             pltpu.VMEM((part, 8, LANES), F32),
             pltpu.VMEM((8 * LANES, (part + 1) * length), BF16),
             pltpu.VMEM((count, length + LANES), F32),
-            pltpu.VMEM((near, 8, length), F32),
+            pltpu.VMEM((2 * near + 1, 8, length), F32),
             pltpu.VMEM((near + 1, LANES), F32),
-            pltpu.VMEM((near + 1, LANES), F32),
+            pltpu.VMEM((2 * near + 2, LANES), F32),
             pltpu.VMEM(((part + 1) * (near + 1), 32, LANES), BF16),
+            pltpu.VMEM((2, 32, LANES), BF16),
             pltpu.VMEM((near + 1, 32, LANES), BF16),
             pltpu.VMEM((count, (part + 1) * length), BF16),
             pltpu.VMEM((8, count, LANES), F32),

time: 61 us -> 59.2 us (0.970)
  Pallas kernels: 59 us -> 57.2 us
    pallas_call x1, Pallas kernels: 59 us -> 57.2 us  [shards(): pl.pallas_call(kernel, out_shape=(jax.ShapeDtypeStruct((count, length), B...]
where the time goes in v8:
time: 59.2 us; the launch traced here: 59.1 us
  Pallas kernels  57.2 us (97%)
  local copies, waits for them, and re-layouts  1.27 us (2%)
  between operations  0.64 us (1%)
    pallas_call x1, Pallas kernels, shards(): pl.pallas_call(kernel, out_shape=(jax.ShapeDtypeStruct((count, length), B...  57.2 us
    unnamed x2, local copies, waits for them, and re-layouts  1.27 us

profile of v8, /device:TPU:1, one launch (start us, length us, event | category | flops | bytes accessed | tf_op | source)
XLA Modules:
  0.0 59.1 jit_solution(11360420614816045819)
XLA Ops:
  0.6 57.2 %separate.1 = (bf16[128,384]{1,0:T(8,128)(2,1)S(1)}, f32[128,128]{1,0:T(8,128)S(1)}) custom-call(bf16[256,384]{1,0:T(8,128)(2,1)} %sig_hbm.1, bf16[128,4096]{1,0:T(8,128)(2,1)} %vec_hbm.1), custom_call_target="tpu_custom_call" | custom-call | flops 1000000000 | bytes 2000000 | tf_op jit(solution)/shard_map/separate/pallas_call | solution.py:458
  57.8 0.6 %copy.6 = bf16[128,384]{1,0:T(8,128)(2,1)} copy(bf16[128,384]{1,0:T(8,128)(2,1)S(1)} %get-tuple-element.4) | data formatting | bytes 196608
  58.5 0.6 %copy.7 = f32[128,128]{1,0:T(8,128)} copy(f32[128,128]{1,0:T(8,128)S(1)} %get-tuple-element.5) | data formatting | bytes 131072

commit v9 on v8

--- a/solution.py
+++ b/solution.py
@@ -30,7 +30,6 @@
 
 
 ELEC, PLANE, RING = moves("x", "h"), moves("x", "h", "l"), moves("z")
-PART = [dict(c=1), dict(l=1), dict(l=1, c=1)]
 ROW, SHEET = moves("x", "l"), moves("z", "h")
 
 
@@ -70,7 +69,7 @@
     )
 
 
-(TAIL, FAR, LATE, SUM, SPILL, CUBE, CROSS, CORE1, CORE2, WAVE, GRAD, GRAM1, GRAM2, GRAM3) = range(14)
+(TAIL, FAR, LATE, SUM, SPILL, CUBE, CROSS, WAVE, GRAD, FRESH, GRAM1, GRAM2, GRAM3) = range(13)
 
 
 def halves(a):
@@ -107,9 +106,9 @@
 
 def kernel(
     sig_hbm, vec_hbm, sources, unmixing,
-    sig, vec, wide, tail_out, tail_in, ext, far_out, far_in, late_out, late_in, feat,
+    sig, vec, tail_out, tail_in, ext, far_in, late_in, feat,
     partial, summed, spill_out, spill_in, blocks, wave_out, waves, cubes,
-    half, grad_out, grad_in, gram, gram_row, gram_sum, gram_sheet, gram_all,
+    half, grad_out, grad_in, fresh_out, fresh, gram, gram_row, gram_sum, gram_sheet, gram_all,
     load, sent, got,
 ):
     at = place()
@@ -148,15 +147,13 @@
             to = moved(at, move)
             greet({"elec": elec_of(to), "tm": (tm + 30) & 31})
             greet(device(to | dict(c=0)))
-        for move in PLANE:
+        for move in PLANE + RING:
             greet(device(moved(at, move)))
+        greet(device(moved(at, dict(l=1, c=1))))
 
     @pl.when(core == 0)
     def _():
         greet({"elec": elec, "tm": before})
-
-    for move in RING + PART:
-        greet(device(moved(at, move)))
 
     lane = lax.broadcasted_iota(jnp.int32, (LAGS, LANES), 1)
     late = lax.broadcasted_iota(jnp.int32, (LAGS, LANES), 0)
@@ -176,15 +173,14 @@
     loads[1].wait()
     partial[...] = dot(vec[...], ext[...])
     spill_out[...] = jnp.concatenate([packed(partial[8 * k : 8 * k + 8, length:], 0) for k in range(16)], 0)
-    every = len(RING) + len(PART) + len(ELEC) + 1
-
-    @pl.when(core == 1)
-    def _():
-        pl.semaphore_wait(barrier, every + len(PLANE) + 1)
-
-    @pl.when(core == 0)
-    def _():
-        pl.semaphore_wait(barrier, every)
+
+    @pl.when(core == 1)
+    def _():
+        pl.semaphore_wait(barrier, len(ELEC) + 1 + len(PLANE) + len(RING) + 1)
+
+    @pl.when(core == 0)
+    def _():
+        pl.semaphore_wait(barrier, len(ELEC) + 2)
 
     onward = (tm + 1 + core) & 31
     for i, move in enumerate(ELEC + [{}]):
@@ -200,51 +196,41 @@
             pl.when(core == 0)(send_sum)
         over = {"elec": elec_of(to), "tm": onward}
         send(spill_out.at[pl.ds(elec_of(to), 1)], spill_in.at[pl.ds(i + 16 * (1 - core), 1)], SPILL, over)
-    wide[...] = sig[...].astype(F32)
     last = lax.broadcasted_iota(jnp.int32, (8, LANES), 1) >= LANES - LAGS
+    ends = sig[:, length - LANES :].astype(F32)
     tail_out[...] = jnp.concatenate(
-        [
-            packed(jnp.where(last, wide[8 * k : 8 * k + 8, length - LANES :], 0.0), LAGS)
-            for k in range(wide.shape[0] // 8)
-        ],
-        0,
+        [packed(jnp.where(last, ends[8 * k : 8 * k + 8], 0.0), LAGS) for k in range(ends.shape[0] // 8)], 0
     )
     send(tail_out, tail_in, TAIL, {"elec": elec, "tm": after})
 
-    def start_of(to, z):
-        return to["l"] * 16 + z * 2 + to["c"]
-
-    for i, move in enumerate(PART):
-        to = moved(at, move)
-        starts = [pl.multiple_of(start_of(to, z) * 8, 8) for z in range(8)]
-        far_out[i] = jnp.concatenate([wide[pl.ds(start, 8), :] for start in starts], 0).astype(BF16)
-    for z in range(8):
-        own = pl.multiple_of(start_of(at, z) * LANES, LANES)
-        feat[z * LANES : (z + 1) * LANES, :length] = ext[pl.ds(own, LANES), :length]
+    other = moved(at, dict(l=1)) | dict(c=1)
+    here = pl.ds(pl.multiple_of(at["l"] * 128, 128), 128)
+    there = pl.ds(pl.multiple_of(other["l"] * 128, 128), 128)
 
     @pl.when(core == 0)
     def _():
         left(SUM, summed.at[pl.ds(0, 16)])
+        send(sig.at[here], far_in.at[0], FAR, partner)
 
     @pl.when(core == 1)
     def _():
         left(SUM, summed.at[pl.ds(0, 15)])
 
-    for i, move in enumerate(PART):
-        send(far_out.at[i], far_in.at[i], FAR, device(moved(at, move)))
+    send(sig.at[there], far_in.at[2 - core], FAR, device(other))
     came(TAIL, tail_in)
-    first = jnp.where(tm > 0, 1.0, 0.0)
-    for i, move in enumerate(PART):
-        to = moved(at, move)
-        late_out[i] = jnp.concatenate([tail_in[pl.ds(start_of(to, z), 1), :] for z in range(8)], 0) * first
-        send(late_out.at[i], late_in.at[i], LATE, device(to))
-
-    @pl.loop(0, 8)
-    def _(z):
-        row = tail_in[pl.ds(start_of(at, z), 1), :] * first
-        for r in range(8):
-            to = pl.ds((z * 8 + r) * LAGS, LAGS)
-            feat[to, :LANES] = jnp.where(spill, before_first(row, r), feat[to, :LANES].astype(F32)).astype(BF16)
+
+    @pl.when((core == 0) & (tm == 0))
+    def _():
+        tail_in[...] = jnp.zeros_like(tail_in)
+
+    here_ends = pl.ds(pl.multiple_of(at["l"] * 16, 16), 16)
+    there_ends = pl.ds(pl.multiple_of(other["l"] * 16, 16), 16)
+
+    @pl.when(core == 0)
+    def _():
+        send(tail_in.at[here_ends], late_in.at[0], LATE, partner)
+
+    send(tail_in.at[there_ends], late_in.at[2 - core], LATE, device(other))
 
     def stacked(block, last):
         return jnp.concatenate([block[:, k * LANES : (k + 1) * LANES] for k in range(tiles)] + [last], 0).astype(BF16)
@@ -280,24 +266,10 @@
                 send(blocks.at[own], blocks.at[pl.ds(2 * elec + 32, 2)], CROSS, device(moved(at, move)))
         waves[elec] = wave_out[1]
 
-    came(FAR, far_in)
-    came(LATE, late_in)
-    for i in range(len(PART)):
-
-        @pl.loop(0, 4)
-        def _(block):
-            rows = far_in[i, pl.ds(block * 16, 16), :].astype(F32)
-            ends = late_in[i, pl.ds(block * 2, 2), :]
-            for r in range(16):
-                to = pl.ds((block * 16 + r) * LAGS, LAGS)
-                turned = [before_first(ends[r // 8 : r // 8 + 1], r % 8)]
-                turned += [lagged(rows[r : r + 1, k * LANES : (k + 1) * LANES]) for k in range(tiles)]
-                for k in range(tiles):
-                    begin = (i + 1) * length + k * LANES
-                    feat[to, begin : begin + LANES] = jnp.where(spill, turned[k], turned[k + 1]).astype(BF16)
+    both = (((1,), (1,)), ((), ()))
 
     def unpack(shard):
-        begin_at = 32 * (shard // 2) + (1 - core if shard % 2 else core)
+        begin_at = 32 * (shard // 2) + 1 - shard % 2
         pads = []
         for pair in range(8):
             pieces = [blocks[begin_at + 2 * (2 * pair + k)].astype(F32) for k in range(2)]
@@ -308,92 +280,77 @@
             pads += [piece[8 * tiles :] for piece in pieces]
         return jnp.concatenate(pads, 0)
 
-    both = (((1,), (1,)), ((), ()))
-    near, far = pl.ds(0, 32), pl.ds(32, 32)
-
-    @pl.when(core == 1)
-    def _():
+    @pl.when(core == 1)
+    def _():
+        feat[:, :length] = ext[pl.ds(pl.multiple_of(at["l"] * 2048, 2048), 2048), :length]
+
+        @pl.loop(0, 8)
+        def _(block):
+            ends = tail_in[pl.ds(at["l"] * 16 + block * 2, 2), :]
+            for r in range(16):
+                to = pl.ds((block * 16 + r) * LAGS, LAGS)
+                turned = before_first(ends[r // 8 : r // 8 + 1], r % 8)
+                feat[to, :LANES] = jnp.where(spill, turned, feat[to, :LANES].astype(F32)).astype(BF16)
+
+        came(FAR, far_in)
+        came(LATE, late_in)
+        for i in range(3):
+
+            @pl.loop(0, 8)
+            def _(block):
+                rows = far_in[i, pl.ds(block * 16, 16), :].astype(F32)
+                ends = late_in[i, pl.ds(block * 2, 2), :]
+                for r in range(16):
+                    to = pl.ds((block * 16 + r) * LAGS, LAGS)
+                    turned = [before_first(ends[r // 8 : r // 8 + 1], r % 8)]
+                    turned += [lagged(rows[r : r + 1, k * LANES : (k + 1) * LANES]) for k in range(tiles)]
+                    for k in range(tiles):
+                        begin = (i + 1) * length + k * LANES
+                        feat[to, begin : begin + LANES] = jnp.where(spill, turned[k], turned[k + 1]).astype(BF16)
+
         came(CUBE, blocks.at[pl.ds(0, 30)])
-        send(blocks.at[near], blocks.at[near], CORE1, partner)
-
-    @pl.when(core == 0)
-    def _():
-        came(CORE1, blocks.at[near])
-
-    pads = unpack(0) + unpack(1)
-    for z in range(8):
-        half[z] = dot(cubes[:, : 2 * length], feat[z * LANES : (z + 1) * LANES, : 2 * length], both)
-
-    @pl.when(core == 1)
-    def _():
-        came(CROSS, blocks.at[far])
-        send(blocks.at[far], blocks.at[far], CORE2, partner)
-
-    @pl.when(core == 0)
-    def _():
-        came(CORE2, blocks.at[far])
-
-    pads = pads + unpack(2) + unpack(3)
-    deriv = jnp.sum(pads, axis=1, keepdims=True)
-
-    def block_of(z):
-        rows = pl.ds(pl.multiple_of(z * LANES, LANES), LANES)
-        columns = pl.ds(pl.multiple_of((at["l"] * 16 + z * 2 + at["c"]) * LANES, LANES), LANES)
-        grad = half[z] + dot(cubes[:, 2 * length :], feat[rows, 2 * length :], both)
-        return grad - deriv * vec[:, columns].astype(F32)
-
-    for i, move in enumerate(RING):
-        to = moved(at, move)
-        grad_out[i] = block_of(to["z"]).astype(BF16)
-        send(grad_out.at[i], grad_in.at[i], GRAD, device(to))
-
-    @pl.when(core == 1)
-    def _():
+        pads = unpack(0) + unpack(1)
+        for z in range(8):
+            half[z] = dot(cubes[:, : 2 * length], feat[z * 256 : z * 256 + 256, : 2 * length], both)
+        came(CROSS, blocks.at[pl.ds(32, 32)])
+        pads = pads + unpack(2) + unpack(3)
+        deriv = jnp.sum(pads, axis=1, keepdims=True)
+
+        def block_of(z):
+            rows = pl.ds(pl.multiple_of(z * 256, 256), 256)
+            columns = pl.ds(pl.multiple_of((at["l"] * 8 + z) * 256, 256), 256)
+            grad = half[z] + dot(cubes[:, 2 * length :], feat[rows, 2 * length :], both)
+            return grad - deriv * vec[:, columns].astype(F32)
+
+        for i, move in enumerate(RING):
+            to = moved(at, move)
+            grad_out[i] = block_of(to["z"]).astype(BF16)
+            send(grad_out.at[i], grad_in.at[i], GRAD, device(to))
         for move in ELEC + [{}]:
             send(wave_out.at[0], waves.at[elec], WAVE, device(moved(at, move) | dict(c=0)))
         for move in ELEC:
             send(wave_out.at[1], waves.at[elec], WAVE, device(moved(at, move)))
-
-    updated = block_of(at["z"])
-
-    @pl.when(core == 0)
-    def _():
-        came(WAVE, waves)
-
-    @pl.when(core == 1)
-    def _():
-        came(WAVE, waves.at[pl.ds(0, len(ELEC))])
-
-    for pair in range(8):
-        pieces = [waves[2 * pair + k].astype(F32) for k in range(2)]
-        for k in range(tiles):
-            rows = jnp.concatenate([piece[8 * k : 8 * k + 8] for piece in pieces], 0)
-            sources[16 * pair : 16 * pair + 16, k * LANES : (k + 1) * LANES] = rows.astype(BF16)
-    came(GRAD, grad_in)
-    for i in range(len(RING)):
-        updated = updated + grad_in[i].astype(F32)
-    updated = updated * (1.0 / (length * 32))
-
-    gram[...] = fine_gram(updated)
+        updated = block_of(at["z"])
+        came(GRAD, grad_in)
+        for i in range(len(RING)):
+            updated = updated + grad_in[i].astype(F32)
+        updated = updated * (1.0 / (length * 32))
+        fresh_out[...] = updated[:, :LANES]
+        fresh[...] = updated[:, LANES:]
+        gram[...] = fine_gram(updated)
+
     mine = pl.ds(pl.multiple_of(row_of(at) * 16, 16), 16)
 
-    def scatter(move, slot):
-        to = moved(at, move) | dict(c=1)
-        rows = pl.ds(pl.multiple_of(row_of(to) * 16, 16), 16)
-        send(gram.at[rows], gram_row.at[slot], GRAM1, device(to))
-
-    for i, move in enumerate(ROW):
-        scatter(move, i + 8 * core)
-
-    @pl.when(core == 0)
-    def _():
-        scatter({}, len(ROW))
-
-    @pl.when(core == 1)
-    def _():
+    @pl.when(core == 1)
+    def _():
+        for i, move in enumerate(ROW):
+            to = moved(at, move)
+            rows = pl.ds(pl.multiple_of(row_of(to) * 16, 16), 16)
+            send(gram.at[rows], gram_row.at[i], GRAM1, device(to))
+        send(fresh_out, fresh, FRESH, partner)
         came(GRAM1, gram_row)
         total = gram[mine, :]
-        for i in range(2 * len(ROW) + 1):
+        for i in range(len(ROW)):
             total = total + gram_row[i]
         gram_sum[...] = total.astype(BF16)
         for i, move in enumerate(SHEET):
@@ -412,6 +369,21 @@
     @pl.when(core == 0)
     def _():
         came(GRAM3, gram_all)
+        came(FRESH, fresh)
+
+    @pl.when(core == 0)
+    def _():
+        came(WAVE, waves)
+
+    @pl.when(core == 1)
+    def _():
+        came(WAVE, waves.at[pl.ds(0, len(ELEC))])
+
+    for pair in range(8):
+        pieces = [waves[2 * pair + k].astype(F32) for k in range(2)]
+        for k in range(tiles):
+            rows = jnp.concatenate([piece[8 * k : 8 * k + 8] for piece in pieces], 0)
+            sources[16 * pair : 16 * pair + 16, k * LANES : (k + 1) * LANES] = rows.astype(BF16)
 
     g = gram_all[...]
     row = lax.broadcasted_iota(jnp.int32, (LANES, LANES), 0)
@@ -420,7 +392,7 @@
     squares = jnp.sum(jnp.sum(g * unit, axis=1, keepdims=True), axis=0, keepdims=True)
     scale = START * math.sqrt(LANES) * lax.rsqrt(squares + 1e-06)
     g = g * scale * scale
-    current = updated * scale
+    current = fresh[...] * scale
     for step in range(NS_STEPS):
         factor = 1.5 * unit - 0.5 * g
         current = fine_dot(factor, current)
@@ -429,31 +401,31 @@
     unmixing[...] = current
 
     left(TAIL, tail_in)
-    left(FAR, far_in)
-    left(LATE, late_in)
     left(SPILL, spill_out)
-    left(GRAD, grad_in)
-
-    @pl.when(core == 0)
-    def _():
-        left(GRAM1, gram_all)
-
-    @pl.when(core == 1)
-    def _():
-        left(GRAM1, gram_all.at[pl.ds(0, 16 * len(ROW))])
-        left(GRAM2, gram_sheet)
-        left(GRAM3, gram_row)
+
+    @pl.when(core == 0)
+    def _():
+        left(FAR, far_in.at[pl.ds(0, 2)])
+        left(LATE, late_in.at[pl.ds(0, 2)])
+
+    @pl.when(core == 1)
+    def _():
+        left(FAR, far_in.at[0])
+        left(LATE, late_in.at[0])
         left(CUBE, blocks.at[pl.ds(0, 30)])
         left(CROSS, blocks.at[pl.ds(0, 32)])
-        left(CORE1, blocks.at[pl.ds(0, 32)])
-        left(CORE2, blocks.at[pl.ds(0, 32)])
         left(WAVE, blocks.at[pl.ds(0, 31)])
+        left(GRAD, grad_in)
+        left(FRESH, fresh)
+        left(GRAM1, gram_row)
+        left(GRAM2, gram_sheet)
+        left(GRAM3, summed.at[pl.ds(0, 10)])
 
 
 def shards(signals, vectors):
     channels, length = signals.shape
     count, columns = vectors.shape
-    near, ring, part, row, sheet = (len(group) for group in (ELEC, RING, PART, ROW, SHEET))
+    near, ring, row, sheet = (len(group) for group in (ELEC, RING, ROW, SHEET))
     vmem = pl.BlockSpec(memory_space=pltpu.VMEM)
     return pl.pallas_call(
         kernel,
@@ -466,34 +438,33 @@
         scratch_shapes=[
             pltpu.VMEM((channels, length), BF16),
             pltpu.VMEM((count, columns), BF16),
-            pltpu.VMEM((channels, length), F32),
             pltpu.VMEM((channels // 8, LANES), F32),
             pltpu.VMEM((channels // 8, LANES), F32),
             pltpu.VMEM((columns, length + LANES), BF16),
-            pltpu.VMEM((part, 64, length), BF16),
-            pltpu.VMEM((part, 64, length), BF16),
-            pltpu.VMEM((part, 8, LANES), F32),
-            pltpu.VMEM((part, 8, LANES), F32),
-            pltpu.VMEM((8 * LANES, (part + 1) * length), BF16),
+            pltpu.VMEM((3, channels // 2, length), BF16),
+            pltpu.VMEM((3, channels // 16, LANES), F32),
+            pltpu.VMEM((columns // 2, 4 * length), BF16),
             pltpu.VMEM((count, length + LANES), F32),
             pltpu.VMEM((2 * near + 1, 8, length), F32),
             pltpu.VMEM((near + 1, LANES), F32),
             pltpu.VMEM((2 * near + 2, LANES), F32),
-            pltpu.VMEM(((part + 1) * (near + 1), 32, LANES), BF16),
+            pltpu.VMEM((4 * (near + 1), 32, LANES), BF16),
             pltpu.VMEM((2, 32, LANES), BF16),
             pltpu.VMEM((near + 1, 32, LANES), BF16),
-            pltpu.VMEM((count, (part + 1) * length), BF16),
-            pltpu.VMEM((8, count, LANES), F32),
-            pltpu.VMEM((ring, count, LANES), BF16),
-            pltpu.VMEM((ring, count, LANES), BF16),
+            pltpu.VMEM((count, 4 * length), BF16),
+            pltpu.VMEM((8, count, 2 * LANES), F32),
+            pltpu.VMEM((ring, count, 2 * LANES), BF16),
+            pltpu.VMEM((ring, count, 2 * LANES), BF16),
+            pltpu.VMEM((count, LANES), F32),
+            pltpu.VMEM((count, LANES), F32),
             pltpu.VMEM((LANES, LANES), F32),
-            pltpu.VMEM((2 * row + 1, 16, LANES), F32),
+            pltpu.VMEM((row, 16, LANES), F32),
             pltpu.VMEM((16, LANES), BF16),
             pltpu.VMEM((sheet, 16, LANES), BF16),
             pltpu.VMEM((LANES, LANES), F32),
             pltpu.SemaphoreType.DMA((2,)),
-            pltpu.SemaphoreType.DMA((14,)),
-            pltpu.SemaphoreType.DMA((14,)),
+            pltpu.SemaphoreType.DMA((13,)),
+            pltpu.SemaphoreType.DMA((13,)),
         ],
         compiler_params=pltpu.CompilerParams(
             collective_id=0, has_side_effects=True, vmem_limit_bytes=40 * 2**20

time: 59.2 us -> 57.9 us (0.978)
  Pallas kernels: 57.2 us -> 55.8 us
    pallas_call x1, Pallas kernels: 57.2 us -> 55.8 us  [shards(): pl.pallas_call(kernel, out_shape=(jax.ShapeDtypeStruct((count, length), B...]
where the time goes in v9:
time: 57.9 us; the launch traced here: 57.7 us
  Pallas kernels  55.8 us (96%)
  local copies, waits for them, and re-layouts  1.27 us (2%)
  between operations  0.64 us (1%)
    pallas_call x1, Pallas kernels, shards(): pl.pallas_call(kernel, out_shape=(jax.ShapeDtypeStruct((count, length), B...  55.8 us
    unnamed x2, local copies, waits for them, and re-layouts  1.27 us

profile of v9, /device:TPU:1, one launch (start us, length us, event | category | flops | bytes accessed | tf_op | source)
XLA Modules:
  0.0 57.7 jit_solution(4613563340291189392)
XLA Ops:
  0.6 55.8 %separate.1 = (bf16[128,384]{1,0:T(8,128)(2,1)S(1)}, f32[128,128]{1,0:T(8,128)S(1)}) custom-call(bf16[256,384]{1,0:T(8,128)(2,1)} %sig_hbm.1, bf16[128,4096]{1,0:T(8,128)(2,1)} %vec_hbm.1), custom_call_target="tpu_custom_call" | custom-call | flops 1000000000 | bytes 2000000 | tf_op jit(solution)/shard_map/separate/pallas_call | solution.py:430
  56.5 0.6 %copy.6 = bf16[128,384]{1,0:T(8,128)(2,1)} copy(bf16[128,384]{1,0:T(8,128)(2,1)S(1)} %get-tuple-element.4) | data formatting | bytes 196608
  57.1 0.6 %copy.7 = f32[128,128]{1,0:T(8,128)} copy(f32[128,128]{1,0:T(8,128)S(1)} %get-tuple-element.5) | data formatting | bytes 131072

commit v10 on v9

--- a/solution.py
+++ b/solution.py
@@ -69,7 +69,7 @@
     )
 
 
-(TAIL, FAR, LATE, SUM, SPILL, CUBE, CROSS, WAVE, GRAD, FRESH, GRAM1, GRAM2, GRAM3) = range(13)
+(TAIL, FAR, LATE, SUM, SPILL, CUBE, CROSS, DERIV, WAVE0, WAVE1, GRAD, FRESH, GRAM1, GRAM2, GRAM3) = range(15)
 
 
 def halves(a):
@@ -107,7 +107,7 @@
 def kernel(
     sig_hbm, vec_hbm, sources, unmixing,
     sig, vec, tail_out, tail_in, ext, far_in, late_in, feat,
-    partial, summed, spill_out, spill_in, blocks, wave_out, waves, cubes,
+    partial, summed, spill_out, spill_in, blocks, deriv_out, derivs, wave_out, waves, cubes,
     half, grad_out, grad_in, fresh_out, fresh, gram, gram_row, gram_sum, gram_sheet, gram_all,
     load, sent, got,
 ):
@@ -232,8 +232,8 @@
 
     send(tail_in.at[there_ends], late_in.at[2 - core], LATE, device(other))
 
-    def stacked(block, last):
-        return jnp.concatenate([block[:, k * LANES : (k + 1) * LANES] for k in range(tiles)] + [last], 0).astype(BF16)
+    def stacked(block):
+        return jnp.concatenate([block[:, k * LANES : (k + 1) * LANES] for k in range(tiles)], 0)
 
     @pl.when(core == 1)
     def _():
@@ -241,6 +241,7 @@
         lane = lax.broadcasted_iota(jnp.int32, (8, LANES), 1)
         came(SUM, summed)
         came(SPILL, spill_in)
+        deriv, cubed = 0.0, []
         for shard in range(2):
             total = summed[15] if shard == 0 else partial[mine, :length]
             for i in range(len(ELEC)):
@@ -251,34 +252,32 @@
             over = jnp.concatenate([pltpu.roll(over, (LANES - r * LAGS) % LANES, 1) for r in range(8)], 0)
             over = jnp.where(lane < LAGS, over, 0.0)
             total = jnp.concatenate([total[:, :LANES] + over, total[:, LANES:]], 1)
-            deriv = jnp.sum(3.0 * total * total, axis=1, keepdims=True)
-            high = deriv.astype(BF16).astype(F32)
-            middle = (deriv - high).astype(BF16).astype(F32)
-            low = deriv - high - middle
-            pad = jnp.where(lane == 0, high, jnp.where(lane == 1, middle, jnp.where(lane == 2, low, 0.0)))
-            blocks[2 * elec + shard] = stacked(total * total * total, pad)
-            wave_out[shard] = stacked(total, jnp.zeros((8, LANES), F32))
-        own = pl.ds(2 * elec, 2)
+            deriv = deriv + jnp.sum(3.0 * total * total, axis=1, keepdims=True)
+            cubed.append(stacked(total * total * total))
+            wave_out[shard] = jnp.concatenate([stacked(total), jnp.zeros((8, LANES), F32)], 0).astype(BF16)
+        blocks[elec] = jnp.concatenate(cubed, 0).astype(BF16)
         for move in ELEC:
-            send(blocks.at[own], blocks.at[own], CUBE, device(moved(at, move)))
+            send(blocks.at[elec], blocks.at[elec], CUBE, device(moved(at, move)))
         for move in PLANE:
             if move["l"]:
-                send(blocks.at[own], blocks.at[pl.ds(2 * elec + 32, 2)], CROSS, device(moved(at, move)))
+                send(blocks.at[elec], blocks.at[elec + 16], CROSS, device(moved(at, move)))
+        deriv = packed(jnp.where(lane == 0, deriv, 0.0), 0)
+        deriv_out[0:1] = deriv
+        derivs[pl.ds(elec, 1)] = deriv
+        for move in PLANE:
+            row = pl.ds(elec + 16 * move["l"], 1)
+            send(deriv_out.at[pl.ds(0, 1)], derivs.at[row], DERIV, device(moved(at, move)))
         waves[elec] = wave_out[1]
 
     both = (((1,), (1,)), ((), ()))
 
-    def unpack(shard):
-        begin_at = 32 * (shard // 2) + 1 - shard % 2
-        pads = []
+    def unpack(part):
         for pair in range(8):
-            pieces = [blocks[begin_at + 2 * (2 * pair + k)].astype(F32) for k in range(2)]
-            for k in range(tiles):
-                rows = jnp.concatenate([piece[8 * k : 8 * k + 8] for piece in pieces], 0)
-                begin = shard * length + k * LANES
+            pieces = [blocks[16 * part + 2 * pair + k].astype(F32) for k in range(2)]
+            for c, k in itertools.product(range(2), range(tiles)):
+                rows = jnp.concatenate([piece[24 * c + 8 * k : 24 * c + 8 * k + 8] for piece in pieces], 0)
+                begin = (2 * part + 1 - c) * length + k * LANES
                 cubes[16 * pair : 16 * pair + 16, begin : begin + LANES] = rows.astype(BF16)
-            pads += [piece[8 * tiles :] for piece in pieces]
-        return jnp.concatenate(pads, 0)
 
     @pl.when(core == 1)
     def _():
@@ -308,13 +307,18 @@
                         begin = (i + 1) * length + k * LANES
                         feat[to, begin : begin + LANES] = jnp.where(spill, turned[k], turned[k + 1]).astype(BF16)
 
-        came(CUBE, blocks.at[pl.ds(0, 30)])
-        pads = unpack(0) + unpack(1)
+        came(CUBE, blocks.at[pl.ds(0, 15)])
+        unpack(0)
         for z in range(8):
             half[z] = dot(cubes[:, : 2 * length], feat[z * 256 : z * 256 + 256, : 2 * length], both)
-        came(CROSS, blocks.at[pl.ds(32, 32)])
-        pads = pads + unpack(2) + unpack(3)
-        deriv = jnp.sum(pads, axis=1, keepdims=True)
+        came(CROSS, blocks.at[pl.ds(16, 16)])
+        unpack(1)
+        came(DERIV, derivs.at[pl.ds(0, 31)])
+        deriv = derivs[:16] + derivs[16:]
+        deriv = jnp.concatenate([jnp.broadcast_to(deriv[k : k + 1], (8, LANES)) for k in range(16)], 0)
+        place_of = (lax.broadcasted_iota(jnp.int32, (LANES, LANES), 0) & 7) * LAGS
+        lane = lax.broadcasted_iota(jnp.int32, (LANES, LANES), 1)
+        deriv = jnp.sum(jnp.where(lane == place_of, deriv, 0.0), axis=1, keepdims=True)
 
         def block_of(z):
             rows = pl.ds(pl.multiple_of(z * 256, 256), 256)
@@ -327,9 +331,9 @@
             grad_out[i] = block_of(to["z"]).astype(BF16)
             send(grad_out.at[i], grad_in.at[i], GRAD, device(to))
         for move in ELEC + [{}]:
-            send(wave_out.at[0], waves.at[elec], WAVE, device(moved(at, move) | dict(c=0)))
+            send(wave_out.at[0], waves.at[elec], WAVE0, device(moved(at, move) | dict(c=0)))
         for move in ELEC:
-            send(wave_out.at[1], waves.at[elec], WAVE, device(moved(at, move)))
+            send(wave_out.at[1], waves.at[elec], WAVE1, device(moved(at, move)))
         updated = block_of(at["z"])
         came(GRAD, grad_in)
         for i in range(len(RING)):
@@ -373,11 +377,11 @@
 
     @pl.when(core == 0)
     def _():
-        came(WAVE, waves)
-
-    @pl.when(core == 1)
-    def _():
-        came(WAVE, waves.at[pl.ds(0, len(ELEC))])
+        came(WAVE0, waves)
+
+    @pl.when(core == 1)
+    def _():
+        came(WAVE1, waves.at[pl.ds(0, len(ELEC))])
 
     for pair in range(8):
         pieces = [waves[2 * pair + k].astype(F32) for k in range(2)]
@@ -412,9 +416,11 @@
     def _():
         left(FAR, far_in.at[0])
         left(LATE, late_in.at[0])
-        left(CUBE, blocks.at[pl.ds(0, 30)])
-        left(CROSS, blocks.at[pl.ds(0, 32)])
-        left(WAVE, blocks.at[pl.ds(0, 31)])
+        left(CUBE, blocks.at[pl.ds(0, 15)])
+        left(CROSS, blocks.at[pl.ds(0, 16)])
+        left(DERIV, derivs.at[pl.ds(0, 31)])
+        left(WAVE0, waves)
+        left(WAVE1, waves.at[pl.ds(0, len(ELEC))])
         left(GRAD, grad_in)
         left(FRESH, fresh)
         left(GRAM1, gram_row)
@@ -448,7 +454,9 @@
             pltpu.VMEM((2 * near + 1, 8, length), F32),
             pltpu.VMEM((near + 1, LANES), F32),
             pltpu.VMEM((2 * near + 2, LANES), F32),
-            pltpu.VMEM((4 * (near + 1), 32, LANES), BF16),
+            pltpu.VMEM((2 * (near + 1), 48, LANES), BF16),
+            pltpu.VMEM((8, LANES), F32),
+            pltpu.VMEM((2 * (near + 1), LANES), F32),
             pltpu.VMEM((2, 32, LANES), BF16),
             pltpu.VMEM((near + 1, 32, LANES), BF16),
             pltpu.VMEM((count, 4 * length), BF16),
@@ -463,8 +471,8 @@
             pltpu.VMEM((sheet, 16, LANES), BF16),
             pltpu.VMEM((LANES, LANES), F32),
             pltpu.SemaphoreType.DMA((2,)),
-            pltpu.SemaphoreType.DMA((13,)),
-            pltpu.SemaphoreType.DMA((13,)),
+            pltpu.SemaphoreType.DMA((15,)),
+            pltpu.SemaphoreType.DMA((15,)),
         ],
         compiler_params=pltpu.CompilerParams(
             collective_id=0, has_side_effects=True, vmem_limit_bytes=40 * 2**20

time: 57.9 us -> 57.6 us (level)
  no operation moved by 1% of the time
where the time goes in v10:
time: 57.6 us; the launch traced here: 57.5 us
  Pallas kernels  55.6 us (97%)
  local copies, waits for them, and re-layouts  1.27 us (2%)
  between operations  0.64 us (1%)
    pallas_call x1, Pallas kernels, shards(): pl.pallas_call(kernel, out_shape=(jax.ShapeDtypeStruct((count, length), B...  55.6 us
    unnamed x2, local copies, waits for them, and re-layouts  1.27 us

profile of v10, /device:TPU:1, one launch (start us, length us, event | category | flops | bytes accessed | tf_op | source)
XLA Modules:
  0.0 57.5 jit_solution(16005371904404879249)
XLA Ops:
  0.6 55.6 %separate.1 = (bf16[128,384]{1,0:T(8,128)(2,1)S(1)}, f32[128,128]{1,0:T(8,128)S(1)}) custom-call(bf16[256,384]{1,0:T(8,128)(2,1)} %sig_hbm.1, bf16[128,4096]{1,0:T(8,128)(2,1)} %vec_hbm.1), custom_call_target="tpu_custom_call" | custom-call | flops 1000000000 | bytes 2000000 | tf_op jit(solution)/shard_map/separate/pallas_call | solution.py:436
  56.2 0.6 %copy.6 = bf16[128,384]{1,0:T(8,128)(2,1)} copy(bf16[128,384]{1,0:T(8,128)(2,1)S(1)} %get-tuple-element.4) | data formatting | bytes 196608
  56.9 0.6 %copy.7 = f32[128,128]{1,0:T(8,128)} copy(f32[128,128]{1,0:T(8,128)S(1)} %get-tuple-element.5) | data formatting | bytes 131072

commit v11 on v10

--- a/solution.py
+++ b/solution.py
@@ -69,7 +69,7 @@
     )
 
 
-(TAIL, FAR, LATE, SUM, SPILL, CUBE, CROSS, DERIV, WAVE0, WAVE1, GRAD, FRESH, GRAM1, GRAM2, GRAM3) = range(15)
+(TAIL, FAR, FAR0, LATE, LATE0, SUM, SPILL, CUBE, CROSS, DERIV, WAVE0, WAVE1, GRAD, FRESH, GRAM1, GRAM2, GRAM3) = range(17)
 
 
 def halves(a):
@@ -210,7 +210,7 @@
     @pl.when(core == 0)
     def _():
         left(SUM, summed.at[pl.ds(0, 16)])
-        send(sig.at[here], far_in.at[0], FAR, partner)
+        send(sig.at[here], far_in.at[0], FAR0, partner)
 
     @pl.when(core == 1)
     def _():
@@ -228,15 +228,42 @@
 
     @pl.when(core == 0)
     def _():
-        send(tail_in.at[here_ends], late_in.at[0], LATE, partner)
+        send(tail_in.at[here_ends], late_in.at[0], LATE0, partner)
 
     send(tail_in.at[there_ends], late_in.at[2 - core], LATE, device(other))
 
     def stacked(block):
         return jnp.concatenate([block[:, k * LANES : (k + 1) * LANES] for k in range(tiles)], 0)
 
-    @pl.when(core == 1)
-    def _():
+    def lag_far(i):
+        @pl.loop(0, 8)
+        def _(block):
+            rows = far_in[i, pl.ds(block * 16, 16), :].astype(F32)
+            ends = late_in[i, pl.ds(block * 2, 2), :]
+            for r in range(16):
+                to = pl.ds((block * 16 + r) * LAGS, LAGS)
+                turned = [before_first(ends[r // 8 : r // 8 + 1], r % 8)]
+                turned += [lagged(rows[r : r + 1, k * LANES : (k + 1) * LANES]) for k in range(tiles)]
+                for k in range(tiles):
+                    begin = (i + 1) * length + k * LANES
+                    feat[to, begin : begin + LANES] = jnp.where(spill, turned[k], turned[k + 1]).astype(BF16)
+
+    @pl.when(core == 1)
+    def _():
+        feat[:, :length] = ext[pl.ds(pl.multiple_of(at["l"] * 2048, 2048), 2048), :length]
+
+        @pl.loop(0, 8)
+        def _(block):
+            ends = tail_in[pl.ds(at["l"] * 16 + block * 2, 2), :]
+            for r in range(16):
+                to = pl.ds((block * 16 + r) * LAGS, LAGS)
+                turned = before_first(ends[r // 8 : r // 8 + 1], r % 8)
+                feat[to, :LANES] = jnp.where(spill, turned, feat[to, :LANES].astype(F32)).astype(BF16)
+
+        came(FAR0, far_in.at[0])
+        came(LATE0, late_in.at[0])
+        lag_far(0)
+
         mine = pl.ds(pl.multiple_of(elec * 8, 8), 8)
         lane = lax.broadcasted_iota(jnp.int32, (8, LANES), 1)
         came(SUM, summed)
@@ -281,32 +308,10 @@
 
     @pl.when(core == 1)
     def _():
-        feat[:, :length] = ext[pl.ds(pl.multiple_of(at["l"] * 2048, 2048), 2048), :length]
-
-        @pl.loop(0, 8)
-        def _(block):
-            ends = tail_in[pl.ds(at["l"] * 16 + block * 2, 2), :]
-            for r in range(16):
-                to = pl.ds((block * 16 + r) * LAGS, LAGS)
-                turned = before_first(ends[r // 8 : r // 8 + 1], r % 8)
-                feat[to, :LANES] = jnp.where(spill, turned, feat[to, :LANES].astype(F32)).astype(BF16)
-
-        came(FAR, far_in)
-        came(LATE, late_in)
-        for i in range(3):
-
-            @pl.loop(0, 8)
-            def _(block):
-                rows = far_in[i, pl.ds(block * 16, 16), :].astype(F32)
-                ends = late_in[i, pl.ds(block * 2, 2), :]
-                for r in range(16):
-                    to = pl.ds((block * 16 + r) * LAGS, LAGS)
-                    turned = [before_first(ends[r // 8 : r // 8 + 1], r % 8)]
-                    turned += [lagged(rows[r : r + 1, k * LANES : (k + 1) * LANES]) for k in range(tiles)]
-                    for k in range(tiles):
-                        begin = (i + 1) * length + k * LANES
-                        feat[to, begin : begin + LANES] = jnp.where(spill, turned[k], turned[k + 1]).astype(BF16)
-
+        came(FAR, far_in.at[pl.ds(1, 2)])
+        came(LATE, late_in.at[pl.ds(1, 2)])
+        lag_far(1)
+        lag_far(2)
         came(CUBE, blocks.at[pl.ds(0, 15)])
         unpack(0)
         for z in range(8):
@@ -409,8 +414,10 @@
 
     @pl.when(core == 0)
     def _():
-        left(FAR, far_in.at[pl.ds(0, 2)])
-        left(LATE, late_in.at[pl.ds(0, 2)])
+        left(FAR, far_in.at[0])
+        left(FAR0, far_in.at[0])
+        left(LATE, late_in.at[0])
+        left(LATE0, late_in.at[0])
 
     @pl.when(core == 1)
     def _():
@@ -471,8 +478,8 @@
             pltpu.VMEM((sheet, 16, LANES), BF16),
             pltpu.VMEM((LANES, LANES), F32),
             pltpu.SemaphoreType.DMA((2,)),
-            pltpu.SemaphoreType.DMA((15,)),
-            pltpu.SemaphoreType.DMA((15,)),
+            pltpu.SemaphoreType.DMA((17,)),
+            pltpu.SemaphoreType.DMA((17,)),
         ],
         compiler_params=pltpu.CompilerParams(
             collective_id=0, has_side_effects=True, vmem_limit_bytes=40 * 2**20

time: 57.6 us -> 58.6 us (1.017)
  Pallas kernels: 55.6 us -> 56.6 us
    pallas_call x1, Pallas kernels: 55.6 us -> 56.6 us  [shards(): pl.pallas_call(kernel, out_shape=(jax.ShapeDtypeStruct((count, length), B...]
where the time goes in v11:
time: 58.6 us; the launch traced here: 58.5 us
  Pallas kernels  56.6 us (97%)
  local copies, waits for them, and re-layouts  1.27 us (2%)
  between operations  0.64 us (1%)
    pallas_call x1, Pallas kernels, shards(): pl.pallas_call(kernel, out_shape=(jax.ShapeDtypeStruct((count, length), B...  56.6 us
    unnamed x2, local copies, waits for them, and re-layouts  1.27 us

profile of v11, /device:TPU:1, one launch (start us, length us, event | category | flops | bytes accessed | tf_op | source)
XLA Modules:
  0.0 58.5 jit_solution(12315949747043832723)
XLA Ops:
  0.6 56.6 %separate.1 = (bf16[128,384]{1,0:T(8,128)(2,1)S(1)}, f32[128,128]{1,0:T(8,128)S(1)}) custom-call(bf16[256,384]{1,0:T(8,128)(2,1)} %sig_hbm.1, bf16[128,4096]{1,0:T(8,128)(2,1)} %vec_hbm.1), custom_call_target="tpu_custom_call" | custom-call | flops 1000000000 | bytes 2000000 | tf_op jit(solution)/shard_map/separate/pallas_call | solution.py:443
  57.2 0.6 %copy.6 = bf16[128,384]{1,0:T(8,128)(2,1)} copy(bf16[128,384]{1,0:T(8,128)(2,1)S(1)} %get-tuple-element.4) | data formatting | bytes 196608
  57.9 0.6 %copy.7 = f32[128,128]{1,0:T(8,128)} copy(f32[128,128]{1,0:T(8,128)S(1)} %get-tuple-element.5) | data formatting | bytes 131072

commit v12 on v10

--- a/solution.py
+++ b/solution.py
@@ -147,7 +147,12 @@
             to = moved(at, move)
             greet({"elec": elec_of(to), "tm": (tm + 30) & 31})
             greet(device(to | dict(c=0)))
-        for move in PLANE + RING:
+            if move:
+                greet(device(to))
+        for move in PLANE:
+            if move["l"]:
+                greet(device(moved(at, move)))
+        for move in RING:
             greet(device(moved(at, move)))
         greet(device(moved(at, dict(l=1, c=1))))
 
@@ -343,6 +348,13 @@
         fresh[...] = updated[:, LANES:]
         gram[...] = fine_gram(updated)
 
+    def gather_sources():
+        for pair in range(8):
+            pieces = [waves[2 * pair + k].astype(F32) for k in range(2)]
+            for k in range(tiles):
+                rows = jnp.concatenate([piece[8 * k : 8 * k + 8] for piece in pieces], 0)
+                sources[16 * pair : 16 * pair + 16, k * LANES : (k + 1) * LANES] = rows.astype(BF16)
+
     mine = pl.ds(pl.multiple_of(row_of(at) * 16, 16), 16)
 
     @pl.when(core == 1)
@@ -352,6 +364,8 @@
             rows = pl.ds(pl.multiple_of(row_of(to) * 16, 16), 16)
             send(gram.at[rows], gram_row.at[i], GRAM1, device(to))
         send(fresh_out, fresh, FRESH, partner)
+        came(WAVE1, waves.at[pl.ds(0, len(ELEC))])
+        gather_sources()
         came(GRAM1, gram_row)
         total = gram[mine, :]
         for i in range(len(ROW)):
@@ -372,22 +386,10 @@
 
     @pl.when(core == 0)
     def _():
+        came(WAVE0, waves)
+        gather_sources()
+        came(FRESH, fresh)
         came(GRAM3, gram_all)
-        came(FRESH, fresh)
-
-    @pl.when(core == 0)
-    def _():
-        came(WAVE0, waves)
-
-    @pl.when(core == 1)
-    def _():
-        came(WAVE1, waves.at[pl.ds(0, len(ELEC))])
-
-    for pair in range(8):
-        pieces = [waves[2 * pair + k].astype(F32) for k in range(2)]
-        for k in range(tiles):
-            rows = jnp.concatenate([piece[8 * k : 8 * k + 8] for piece in pieces], 0)
-            sources[16 * pair : 16 * pair + 16, k * LANES : (k + 1) * LANES] = rows.astype(BF16)
 
     g = gram_all[...]
     row = lax.broadcasted_iota(jnp.int32, (LANES, LANES), 0)

time: 57.6 us -> 57.3 us (level)
  no operation moved by 1% of the time
where the time goes in v12:
time: 57.3 us; the launch traced here: 57.2 us
  Pallas kernels  55.3 us (97%)
  local copies, waits for them, and re-layouts  1.27 us (2%)
  between operations  0.64 us (1%)
    pallas_call x1, Pallas kernels, shards(): pl.pallas_call(kernel, out_shape=(jax.ShapeDtypeStruct((count, length), B...  55.3 us
    unnamed x2, local copies, waits for them, and re-layouts  1.27 us

profile of v12, /device:TPU:1, one launch (start us, length us, event | category | flops | bytes accessed | tf_op | source)
XLA Modules:
  0.0 57.2 jit_solution(7802295803713591445)
XLA Ops:
  0.6 55.3 %separate.1 = (bf16[128,384]{1,0:T(8,128)(2,1)S(1)}, f32[128,128]{1,0:T(8,128)S(1)}) custom-call(bf16[256,384]{1,0:T(8,128)(2,1)} %sig_hbm.1, bf16[128,4096]{1,0:T(8,128)(2,1)} %vec_hbm.1), custom_call_target="tpu_custom_call" | custom-call | flops 1000000000 | bytes 2000000 | tf_op jit(solution)/shard_map/separate/pallas_call | solution.py:438
  55.9 0.6 %copy.6 = bf16[128,384]{1,0:T(8,128)(2,1)} copy(bf16[128,384]{1,0:T(8,128)(2,1)S(1)} %get-tuple-element.4) | data formatting | bytes 196608
  56.6 0.6 %copy.7 = f32[128,128]{1,0:T(8,128)} copy(f32[128,128]{1,0:T(8,128)S(1)} %get-tuple-element.5) | data formatting | bytes 131072

commit v13 on v12

--- a/solution.py
+++ b/solution.py
@@ -149,10 +149,7 @@
             greet(device(to | dict(c=0)))
             if move:
                 greet(device(to))
-        for move in PLANE:
-            if move["l"]:
-                greet(device(moved(at, move)))
-        for move in RING:
+        for move in RING + [dict(l=1)]:
             greet(device(moved(at, move)))
         greet(device(moved(at, dict(l=1, c=1))))
 
@@ -181,7 +178,7 @@
 
     @pl.when(core == 1)
     def _():
-        pl.semaphore_wait(barrier, len(ELEC) + 1 + len(PLANE) + len(RING) + 1)
+        pl.semaphore_wait(barrier, 2 * len(ELEC) + len(RING) + 3)
 
     @pl.when(core == 0)
     def _():
@@ -244,6 +241,7 @@
     def _():
         mine = pl.ds(pl.multiple_of(elec * 8, 8), 8)
         lane = lax.broadcasted_iota(jnp.int32, (8, LANES), 1)
+        came(FAR, far_in)
         came(SUM, summed)
         came(SPILL, spill_in)
         deriv, cubed = 0.0, []
@@ -296,7 +294,6 @@
                 turned = before_first(ends[r // 8 : r // 8 + 1], r % 8)
                 feat[to, :LANES] = jnp.where(spill, turned, feat[to, :LANES].astype(F32)).astype(BF16)
 
-        came(FAR, far_in)
         came(LATE, late_in)
         for i in range(3):
 

time: 57.3 us -> 58.6 us (1.023)
  Pallas kernels: 55.3 us -> 56.6 us
    pallas_call x1, Pallas kernels: 55.3 us -> 56.6 us  [shards(): pl.pallas_call(kernel, out_shape=(jax.ShapeDtypeStruct((count, length), B...]
where the time goes in v13:
time: 58.6 us; the launch traced here: 58.5 us
  Pallas kernels  56.6 us (97%)
  local copies, waits for them, and re-layouts  1.27 us (2%)
  between operations  0.64 us (1%)
    pallas_call x1, Pallas kernels, shards(): pl.pallas_call(kernel, out_shape=(jax.ShapeDtypeStruct((count, length), B...  56.6 us
    unnamed x2, local copies, waits for them, and re-layouts  1.27 us

profile of v13, /device:TPU:1, one launch (start us, length us, event | category | flops | bytes accessed | tf_op | source)
XLA Modules:
  0.0 58.5 jit_solution(9752082729254561010)
XLA Ops:
  0.6 56.6 %separate.1 = (bf16[128,384]{1,0:T(8,128)(2,1)S(1)}, f32[128,128]{1,0:T(8,128)S(1)}) custom-call(bf16[256,384]{1,0:T(8,128)(2,1)} %sig_hbm.1, bf16[128,4096]{1,0:T(8,128)(2,1)} %vec_hbm.1), custom_call_target="tpu_custom_call" | custom-call | flops 1000000000 | bytes 2000000 | tf_op jit(solution)/shard_map/separate/pallas_call | solution.py:435
  57.2 0.6 %copy.6 = bf16[128,384]{1,0:T(8,128)(2,1)} copy(bf16[128,384]{1,0:T(8,128)(2,1)S(1)} %get-tuple-element.4) | data formatting | bytes 196608
  57.8 0.6 %copy.7 = f32[128,128]{1,0:T(8,128)} copy(f32[128,128]{1,0:T(8,128)S(1)} %get-tuple-element.5) | data formatting | bytes 131072

commit v14 on v12

--- a/solution.py
+++ b/solution.py
@@ -166,11 +166,11 @@
 
     loads[0].wait()
 
-    @pl.loop(0, 16)
+    @pl.loop(0, 8)
     def _(block):
-        rows = sig[pl.ds(block * 16, 16), :].astype(F32)
-        for r in range(16):
-            to = pl.ds((block * 16 + r) * LAGS, LAGS)
+        rows = sig[pl.ds(block * 32, 32), :].astype(F32)
+        for r in range(32):
+            to = pl.ds((block * 32 + r) * LAGS, LAGS)
             turned = [lagged(rows[r : r + 1, k * LANES : (k + 1) * LANES]) for k in range(tiles)]
             for k, (a, b) in enumerate(zip([0.0] + turned, turned + [0.0])):
                 ext[to, k * LANES : (k + 1) * LANES] = jnp.where(spill, a, b).astype(BF16)
@@ -300,12 +300,12 @@
         came(LATE, late_in)
         for i in range(3):
 
-            @pl.loop(0, 8)
+            @pl.loop(0, 4)
             def _(block):
-                rows = far_in[i, pl.ds(block * 16, 16), :].astype(F32)
-                ends = late_in[i, pl.ds(block * 2, 2), :]
-                for r in range(16):
-                    to = pl.ds((block * 16 + r) * LAGS, LAGS)
+                rows = far_in[i, pl.ds(block * 32, 32), :].astype(F32)
+                ends = late_in[i, pl.ds(block * 4, 4), :]
+                for r in range(32):
+                    to = pl.ds((block * 32 + r) * LAGS, LAGS)
                     turned = [before_first(ends[r // 8 : r // 8 + 1], r % 8)]
                     turned += [lagged(rows[r : r + 1, k * LANES : (k + 1) * LANES]) for k in range(tiles)]
                     for k in range(tiles):

time: 57.3 us -> 57.3 us (level)
  no operation moved by 1% of the time
where the time goes in v14:
time: 57.3 us; the launch traced here: 57.1 us
  Pallas kernels  55.2 us (96%)
  local copies, waits for them, and re-layouts  1.27 us (2%)
  between operations  0.64 us (1%)
    pallas_call x1, Pallas kernels, shards(): pl.pallas_call(kernel, out_shape=(jax.ShapeDtypeStruct((count, length), B...  55.2 us
    unnamed x2, local copies, waits for them, and re-layouts  1.27 us

profile of v14, /device:TPU:1, one launch (start us, length us, event | category | flops | bytes accessed | tf_op | source)
XLA Modules:
  0.0 57.1 jit_solution(16286071832078331732)
XLA Ops:
  0.6 55.2 %separate.1 = (bf16[128,384]{1,0:T(8,128)(2,1)S(1)}, f32[128,128]{1,0:T(8,128)S(1)}) custom-call(bf16[256,384]{1,0:T(8,128)(2,1)} %sig_hbm.1, bf16[128,4096]{1,0:T(8,128)(2,1)} %vec_hbm.1), custom_call_target="tpu_custom_call" | custom-call | flops 1000000000 | bytes 2000000 | tf_op jit(solution)/shard_map/separate/pallas_call | solution.py:438
  55.9 0.6 %copy.6 = bf16[128,384]{1,0:T(8,128)(2,1)} copy(bf16[128,384]{1,0:T(8,128)(2,1)S(1)} %get-tuple-element.4) | data formatting | bytes 196608
  56.5 0.6 %copy.7 = f32[128,128]{1,0:T(8,128)} copy(f32[128,128]{1,0:T(8,128)S(1)} %get-tuple-element.5) | data formatting | bytes 131072
